TPU v7x, 32 devices: a whole 2x2x4 slice. The times are simulated.
32 devices in a mesh: sec: 2 (over y), gx: 4 (over z), gy: 4 (over x, core).
Axes of the slice: x: 2, y: 2, z: 4, core: 2. Of those that a mesh axis runs over, the one named last changes fastest.
Arguments:
- ocean_velocity: float32 [2, 8, 256, 1024], P(None, None, 'gx', ('sec', 'gy')), may hold values from -6 to 6
- wind_stress: float32 [2, 256, 1024], P(None, 'gx', ('sec', 'gy')), may hold values from -6 to 6
- level_counts: int32 [256, 1024], P('gx', ('sec', 'gy')), may hold values from 1 to 8
- floe_position: float32 [4, 8, 2, 2048], P('gx', ('sec', 'gy')), may hold values from 0 to 4
- floe_velocity: float32 [4, 8, 2, 2048], P('gx', ('sec', 'gy')), may hold values from -3 to 3
- floe_radius: float32 [4, 8, 2048], P('gx', ('sec', 'gy')), may hold values from 0.5 to 1.5
- floe_mass: float32 [4, 8, 2048], P('gx', ('sec', 'gy')), may hold values from 0.5 to 5
- floe_polygon: float32 [4, 8, 32, 2048], P('gx', ('sec', 'gy')), may hold values from -2 to 2
- remap_cells: int32 [4, 8, 2048], P('gx', ('sec', 'gy')), may hold values from 0 to 32767, as said below
- contact_count: int32 [4, 8], P('gx', ('sec', 'gy')), may hold values from 8 to 64, as said below
- contact_list: int32 [4, 8, 3, 64], P('gx', ('sec', 'gy')), may hold values from 0 to 15, as said below
- move_index: int32 [4, 8, 8, 128], P('gx', ('sec', 'gy')), may hold values from 0 to 2047, as said below
- move_count: int32 [4, 8, 8], P('gx', ('sec', 'gy')), may hold values from 42 to 128, as said below
Outputs:
- ocean_next: float32 [2, 8, 256, 1024], P(None, None, 'gx', ('sec', 'gy'))
- floe_next: float32 [4, 8, 4, 2048], P('gx', ('sec', 'gy'))
- arrivals: float32 [4, 8, 8, 38, 128], P('gx', ('sec', 'gy'))
Inputs may be any that keep to these rules, and one draw needn't show every extreme that they name: `contact_list`: row 0 of each slot names a block of the tile, 0 to 15; row 1 a source 0 to 8, 4 meaning the tile itself; row 2 a block of the source: 0 to 15 for source 4, else 0 to 3. Only the first contact_count slots count. `contact_count`: some tile uses all 64 slots in every draw. `move_index`: the floes named by one tile over all directions and slots are distinct. `move_count`: every tile fills all 128 slots towards at least one neighbour. `remap_cells`: Row-major index over the 256 rows and the tile's 128 columns. The floes of tile row i lie in grid rows i * 64 - 64 // 2 to i * 64 + 64 + 64 // 2 - 1 (within the grid), and every tile has floes in the first and the last row of that band.
All inputs are finite; a program needn't handle non-finite values.
Results may differ from a plain program's by a relative error of at most 0.0003.
Values sent between devices are 32-bit elements; how exact they have to be, the bound alone decides.
A program may use at most 64 MiB of HBM per device.

v0:
```python
import math

import jax
import jax.numpy as jnp
from jax import lax
from jax.sharding import PartitionSpec as P

OSTEPS = 4
GHOST = 4


SOFTEN = 0.1
STIFFNESS = 0.1
DAMPING = 0.05
VERT_MIX = 0.15
CORIOLIS = 0.1
SURFACE_GAIN = 0.25
WATER_DRAG = 0.1
AIR_GAIN = 0.2
ICE_STEP = 0.5
PLACES = (0, 1, 2, 3, 5, 6, 7, 8)


def with_halo(array, sides, width):
    for axis, dim in sides:
        size, length = (lax.axis_size(axis), array.shape[dim])
        up = [(i, (i + 1) % size) for i in range(size - 1)]
        down = [(j, i) for i, j in up]
        last = lax.slice_in_dim(array, length - width, length, axis=dim)
        leading = lax.slice_in_dim(array, 0, width, axis=dim)
        before = lax.ppermute(last, axis, up)
        after = lax.ppermute(leading, axis, down)
        array = jnp.concatenate([before, array, after], axis=dim)
    return array


def ocean_substep(flow, padded, wet, wind):
    levels_here = flow.shape[1]
    lap = (
        padded[:, :, :-2, 1:-1]
        + padded[:, :, 2:, 1:-1]
        + padded[:, :, 1:-1, :-2]
        + padded[:, :, 1:-1, 2:]
        - 4.0 * flow
    )
    depth = jnp.arange(levels_here, dtype=jnp.float32)
    horizontal = (0.15 - 0.05 * depth / levels_here)[None, :, None, None]
    flux = VERT_MIX * (flow[:, 1:] - flow[:, :-1]) * wet[None, 1:]
    empty = jnp.zeros_like(flow[:, :1])
    vert = jnp.concatenate([flux, empty], axis=1) - jnp.concatenate([empty, flux], axis=1)
    turning = jnp.stack([CORIOLIS * flow[1], -CORIOLIS * flow[0]])
    surface = jnp.concatenate([SURFACE_GAIN * wind[:, None], jnp.zeros_like(flow[:, 1:])], axis=1)
    return (flow + horizontal * lap + vert + turning + surface) * wet[None]


def pair_forces(first, second):
    delta_x = first[:, 0, :, None] - second[:, 0, None, :]
    delta_y = first[:, 1, :, None] - second[:, 1, None, :]
    distance = jnp.sqrt(delta_x * delta_x + delta_y * delta_y + SOFTEN * SOFTEN)
    reach = first[:, 4, :, None] + second[:, 4, None, :]
    intersection = jnp.maximum(reach - distance, 0.0)
    reduced = first[:, 4, :, None] * second[:, 4, None, :] / reach
    normal_x = delta_x / distance
    normal_y = delta_y / distance
    closing = (first[:, 2, :, None] - second[:, 2, None, :]) * normal_x + (
        first[:, 3, :, None] - second[:, 3, None, :]
    ) * normal_y
    magnitude = intersection * reduced * (STIFFNESS - DAMPING * closing)
    return jnp.stack(
        [jnp.sum(magnitude * normal_x, axis=2), jnp.sum(magnitude * normal_y, axis=2)], axis=1
    )


def block_table(own, ghosts):
    blocks = own.shape[1] // 128
    edge_blocks = ghosts.shape[2] // 128
    mine = own.reshape(5, blocks, 128).transpose(1, 0, 2)
    theirs = (
        ghosts.reshape(8, 5, edge_blocks, 128)
        .transpose(0, 2, 1, 3)
        .reshape(8 * edge_blocks, 5, 128)
    )
    return jnp.concatenate([mine, theirs], axis=0)


def contact_batch(table, lists, valid, blocks, edge_blocks):
    source = lists[1]
    neighbour = source - (source > 4).astype(jnp.int32)
    partner = jnp.where(source == 4, lists[2], blocks + neighbour * edge_blocks + lists[2])
    forces = pair_forces(table[lists[0]], table[partner])
    forces = jnp.where(valid[:, None, None], forces, 0.0)
    onehot = (lists[0][:, None] == jnp.arange(blocks, dtype=jnp.int32)[None, :]).astype(jnp.float32)
    return jnp.einsum("pn,pcf->ncf", onehot, forces, precision=lax.Precision.HIGHEST)


def shards(
    ocean_velocity,
    wind_stress,
    level_counts,
    floe_position,
    floe_velocity,
    floe_radius,
    floe_mass,
    floe_polygon,
    remap_cells,
    contact_count,
    contact_list,
    move_index,
    move_count,
):
    levels_here = ocean_velocity.shape[1]
    rows_here = ocean_velocity.shape[2]
    cols_here = ocean_velocity.shape[3]
    wet = (jnp.arange(levels_here, dtype=jnp.int32)[:, None, None] < level_counts[None]).astype(
        jnp.float32
    )
    flow = ocean_velocity * wet[None]
    for substep in range(OSTEPS):
        padded = with_halo(flow, (("gx", 2), (("sec", "gy"), 3)), 1)
        flow = ocean_substep(flow, padded, wet, wind_stress)
    surface = jnp.stack([flow[0, 0], flow[1, 0], wind_stress[0], wind_stress[1]])
    position = floe_position[0, 0]
    velocity = floe_velocity[0, 0]
    radius = floe_radius[0, 0]
    mass = floe_mass[0, 0]
    cells = remap_cells[0, 0]
    floes = position.shape[1]
    blocks = floes // 128
    record = jnp.concatenate([position, velocity, radius[None]], axis=0)
    edge = record[:, : GHOST * 128]
    beside_all = with_halo(edge[None, None], (("gx", 0), (("sec", "gy"), 1)), 1)
    beside_all = beside_all.reshape(9, 5, GHOST * 128)
    ghosts = jnp.concatenate([beside_all[:4], beside_all[5:]], axis=0)
    table = block_table(record, ghosts)
    margin = rows_here // 2
    near = with_halo(surface, (("gx", 1),), margin)
    first_row = lax.axis_index("gx") * rows_here - margin
    sampled = jnp.take(near.reshape(4, -1), cells - first_row * cols_here, axis=1)
    lists = contact_list[0, 0]
    count = contact_count[0, 0]
    slots = lists.shape[1]
    batch = math.gcd(slots, 32)
    rounds = (count + batch - 1) // batch

    def accumulate(turn, total):
        start = turn * batch
        group = lax.dynamic_slice_in_dim(lists, start, batch, 1)
        valid = start + jnp.arange(batch, dtype=jnp.int32) < count
        return total + contact_batch(table, group, valid, blocks, GHOST)

    contact = lax.fori_loop(0, rounds, accumulate, jnp.zeros((blocks, 2, 128), jnp.float32))
    contact = contact.transpose(1, 0, 2).reshape(2, floes)
    area = math.pi * radius * radius
    relative = sampled[0:2] - velocity
    speed = jnp.sqrt(jnp.sum(relative * relative, axis=0, keepdims=True))
    total = contact + area[None] * (WATER_DRAG * speed * relative + AIR_GAIN * sampled[2:4])
    new_velocity = velocity + ICE_STEP * total / mass[None]
    new_position = position + ICE_STEP * new_velocity
    floe_next = jnp.concatenate([new_position, new_velocity], axis=0)
    rows_all = jnp.concatenate([floe_next, radius[None], mass[None], floe_polygon[0, 0]], axis=0)
    width = rows_all.shape[0]
    leaving = move_index[0, 0]
    capacity = leaving.shape[1]
    taken = (
        jnp.take(rows_all, leaving.reshape(-1), axis=1)
        .reshape(width, 8, capacity)
        .transpose(1, 0, 2)
    )
    valid_slots = jnp.arange(capacity, dtype=jnp.int32)[None, :] < move_count[0, 0][:, None]
    outgoing = jnp.where(valid_slots[:, None, :], taken, 0.0)
    landed = with_halo(outgoing[None, None], (("gx", 0), (("sec", "gy"), 1)), 1)
    landed = landed.reshape(9, 8, width, capacity)
    arrived = [landed[8 - PLACES[way], way] for way in range(8)]
    arrivals = jnp.stack(arrived, axis=0)
    return (flow, floe_next[None, None], arrivals[None, None])


def solution(mesh):
    return jax.shard_map(
        shards,
        mesh=mesh,
        in_specs=(
            P(None, None, "gx", ("sec", "gy")),
            P(None, "gx", ("sec", "gy")),
            P("gx", ("sec", "gy")),
            P("gx", ("sec", "gy"), None, None),
            P("gx", ("sec", "gy"), None, None),
            P("gx", ("sec", "gy"), None),
            P("gx", ("sec", "gy"), None),
            P("gx", ("sec", "gy"), None, None),
            P("gx", ("sec", "gy"), None),
            P("gx", ("sec", "gy")),
            P("gx", ("sec", "gy"), None, None),
            P("gx", ("sec", "gy"), None, None),
            P("gx", ("sec", "gy"), None),
        ),
        out_specs=(
            P(None, None, "gx", ("sec", "gy")),
            P("gx", ("sec", "gy"), None, None),
            P("gx", ("sec", "gy"), None, None, None),
        ),
        check_vma=False,
    )
```

profile of v0, /device:TPU:1, one launch (start us, length us, event | category | flops | bytes accessed | tf_op | source)
XLA Modules:
  0.0 190.8 jit_solution(1121463022658230330)
XLA Ops:
  0.6 1.3 fusion.68
  2.0 4.6 %collective-permute-start.16 = (f32[1,1,5,512]{3,2,1,0:T(8,128)}, f32[1,1,5,512]{3,2,1,0:T(8,128)}, u32[]{:S(2)}, u32[]{:S(2)}) collective-permute-start(f32[1,1,5,512]{3,2,1,0:T(8,128)} %fusion.68), channel_id=1, source_target_pairs={{0,4},{4,8},{8,12},{1,5},{5,9},{9,13},{2,6},{6,10},{10,14},{3,7},{... | collective-permute-start | bytes 30728 | tf_op jit(solution)/shard_map/ppermute | solution.py:31
  8.7 1.4 copy_multiply_fusion
  10.2 4.1 %collective-permute-start = (f32[2,8,1,128]{3,1,2,0:T(8,128)S(1)}, f32[2,8,1,128]{3,1,2,0:T(8,128)S(1)}, u32[]{:S(2)}, u32[]{:S(2)}) collective-permute-start(f32[2,8,1,128]{3,1,2,0:T(8,128)S(1)} %get-tuple-element.122), channel_id=1, source_target_pairs={{0,4},{4,8},{8,12},{1,5},{5,9},{9,13},{2,6},{6,10},{10,14},{3,7},{... | collective-permute-start | bytes 24584 | tf_op jit(solution)/shard_map/ppermute | solution.py:31
  20.9 1.3 copy.208
  22.6 1.4 copy.209
  26.3 4.5 %collective-permute-start.2 = (f32[2,8,66,1]{2,1,3,0:T(8,128)}, f32[2,8,66,1]{2,1,3,0:T(8,128)S(1)}, u32[]{:S(2)}, u32[]{:S(2)}) collective-permute-start(f32[2,8,66,1]{2,1,3,0:T(8,128)} %copy.183), channel_id=1, source_target_pairs={{0,1},{1,2},{2,3},{3,16},{16,17},{17,18},{18,19},{4,5},{5,6},{6,7}... | collective-permute-start | bytes 12680 | tf_op jit(solution)/shard_map/ppermute | solution.py:31
  31.1 1.9 %collective-permute-start.3 = (f32[2,8,66,1]{2,1,3,0:T(8,128)S(1)}, f32[2,8,66,1]{2,1,3,0:T(8,128)S(1)}, u32[]{:S(2)}, u32[]{:S(2)}) collective-permute-start(f32[2,8,66,1]{2,1,3,0:T(8,128)S(1)} %copy.185), channel_id=1, source_target_pairs={{1,0},{2,1},{3,2},{16,3},{17,16},{18,17},{19,18},{5,4},{6,5},{7,6}... | collective-permute-start | bytes 12680 | tf_op jit(solution)/shard_map/ppermute | solution.py:32
  33.0 1.3 copy_dynamic-update-slice_fusion.2
  34.3 1.3 copy_dynamic-update-slice_fusion.1
  35.7 1.3 copy_dynamic-update-slice_fusion
  37.0 3.6 %collective-permute-start.18 = (f32[3,1,5,512]{3,1,2,0:T(1,128)}, f32[3,1,5,512]{3,1,2,0:T(1,128)}, u32[]{:S(2)}, u32[]{:S(2)}) collective-permute-start(f32[3,1,5,512]{3,1,2,0:T(1,128)} %copy_dynamic-update-slice_fusion), channel_id=1, source_target_pairs={{0,1},{1,2},{2,3},{3,16},{16,17},{17,18},{18,19},{4,5},{5,6},{6,7}... | collective-permute-start | bytes 92168 | tf_op jit(solution)/shard_map/ppermute | solution.py:31
  40.6 1.9 %collective-permute-start.19 = (f32[3,1,5,512]{3,1,2,0:T(1,128)}, f32[3,1,5,512]{3,1,2,0:T(1,128)}, u32[]{:S(2)}, u32[]{:S(2)}) collective-permute-start(f32[3,1,5,512]{3,1,2,0:T(1,128)} %copy_dynamic-update-slice_fusion), channel_id=1, source_target_pairs={{1,0},{2,1},{3,2},{16,3},{17,16},{18,17},{19,18},{5,4},{6,5},{7,6}... | collective-permute-start | bytes 92168 | tf_op jit(solution)/shard_map/ppermute | solution.py:32
  44.0 2.0 %fusion.20 = f32[2,8,64,128]{3,1,2,0:T(8,128)S(1)} fusion(f32[2,1,64,128]{3,1,2,0:T(1,128)S(1)} %bitcast.157, f32[2,8,64,128]{3,1,2,0:T(8,128)S(1)} %copy_multiply_fusion, f32[2,8,66,1]{3,1,2,0:T(8,128)} %copy.186, f32[2,8,1,128]{3,1,2,0:T(8,128)} %copy-done.15, f32[2,8,1,128]{3,1,2,0:T(8,128)} %copy-done.14, f32[2,8,66,1]{3,1,2,0:T(8,128)S(1)} %copy.184, ...), kind=kLoop, calls=%fused_computation.52 | loop fusion | flops 2752512 | bytes 2384160 | tf_op jit(solution)/shard_map/mul | solution.py:53
  46.0 4.3 %collective-permute-start.4 = (f32[2,8,1,128]{3,1,2,0:T(8,128)S(1)}, f32[2,8,1,128]{3,1,2,0:T(8,128)S(1)}, u32[]{:S(2)}, u32[]{:S(2)}) collective-permute-start(f32[2,8,1,128]{3,1,2,0:T(8,128)S(1)} %get-tuple-element.118), channel_id=1, source_target_pairs={{0,4},{4,8},{8,12},{1,5},{5,9},{9,13},{2,6},{6,10},{10,14},{3,7},{... | collective-permute-start | bytes 24584 | tf_op jit(solution)/shard_map/ppermute | solution.py:31
  51.6 3.0 %collective-permute-done.5 = f32[2,8,1,128]{3,1,2,0:T(8,128)S(1)} collective-permute-done((f32[2,8,1,128]{3,1,2,0:T(8,128)S(1)}, f32[2,8,1,128]{3,1,2,0:T(8,128)S(1)}, u32[]{:S(2)}, u32[]{:S(2)}) %collective-permute-start.5) | collective-permute-done | bytes 8224 | tf_op jit(solution)/shard_map/ppermute | solution.py:32
  55.7 1.9 copy.187
  57.6 5.1 %collective-permute-start.6 = (f32[2,8,66,1]{2,1,3,0:T(8,128)}, f32[2,8,66,1]{2,1,3,0:T(8,128)}, u32[]{:S(2)}, u32[]{:S(2)}) collective-permute-start(f32[2,8,66,1]{2,1,3,0:T(8,128)} %copy.187), channel_id=1, source_target_pairs={{0,1},{1,2},{2,3},{3,16},{16,17},{17,18},{18,19},{4,5},{5,6},{6,7}... | collective-permute-start | bytes 12680 | tf_op jit(solution)/shard_map/ppermute | solution.py:31
  63.5 1.9 collective-permute-start.7
  66.2 1.8 copy.188
  69.8 1.7 fusion.21
  71.5 2.8 %collective-permute-start.8 = (f32[2,8,1,128]{3,1,2,0:T(8,128)S(1)}, f32[2,8,1,128]{3,1,2,0:T(8,128)S(1)}, u32[]{:S(2)}, u32[]{:S(2)}) collective-permute-start(f32[2,8,1,128]{3,1,2,0:T(8,128)S(1)} %get-tuple-element.114), channel_id=1, source_target_pairs={{0,4},{4,8},{8,12},{1,5},{5,9},{9,13},{2,6},{6,10},{10,14},{3,7},{... | collective-permute-start | bytes 24584 | tf_op jit(solution)/shard_map/ppermute | solution.py:31
  76.5 2.5 %collective-permute-done.9 = f32[2,8,1,128]{3,1,2,0:T(8,128)S(1)} collective-permute-done((f32[2,8,1,128]{3,1,2,0:T(8,128)S(1)}, f32[2,8,1,128]{3,1,2,0:T(8,128)S(1)}, u32[]{:S(2)}, u32[]{:S(2)}) %collective-permute-start.9) | collective-permute-done | bytes 8224 | tf_op jit(solution)/shard_map/ppermute | solution.py:32
  80.2 1.4 copy.191
  81.6 4.1 %collective-permute-start.10 = (f32[2,8,66,1]{2,1,3,0:T(8,128)S(1)}, f32[2,8,66,1]{2,1,3,0:T(8,128)S(1)}, u32[]{:S(2)}, u32[]{:S(2)}) collective-permute-start(f32[2,8,66,1]{2,1,3,0:T(8,128)S(1)} %copy.191), channel_id=1, source_target_pairs={{0,1},{1,2},{2,3},{3,16},{16,17},{17,18},{18,19},{4,5},{5,6},{6,7}... | collective-permute-start | bytes 12680 | tf_op jit(solution)/shard_map/ppermute | solution.py:31
  87.0 1.9 %collective-permute-start.11 = (f32[2,8,66,1]{2,1,3,0:T(8,128)S(1)}, f32[2,8,66,1]{2,1,3,0:T(8,128)S(1)}, u32[]{:S(2)}, u32[]{:S(2)}) collective-permute-start(f32[2,8,66,1]{2,1,3,0:T(8,128)S(1)} %copy.193), channel_id=1, source_target_pairs={{1,0},{2,1},{3,2},{16,3},{17,16},{18,17},{19,18},{5,4},{6,5},{7,6}... | collective-permute-start | bytes 12680 | tf_op jit(solution)/shard_map/ppermute | solution.py:32
  90.7 1.6 collective-permute-done.11
  93.4 1.7 fusion.22
  96.8 3.3 %collective-permute-start.12 = (f32[2,8,1,128]{3,1,2,0:T(8,128)S(1)}, f32[2,8,1,128]{3,1,2,0:T(8,128)S(1)}, u32[]{:S(2)}, u32[]{:S(2)}) collective-permute-start(f32[2,8,1,128]{3,1,2,0:T(8,128)S(1)} %get-tuple-element.110), channel_id=1, source_target_pairs={{0,4},{4,8},{8,12},{1,5},{5,9},{9,13},{2,6},{6,10},{10,14},{3,7},{... | collective-permute-start | bytes 24584 | tf_op jit(solution)/shard_map/ppermute | solution.py:31
  103.1 1.4 collective-permute-done.13
  106.3 5.1 %collective-permute-start.14 = (f32[2,8,66,1]{2,1,3,0:T(8,128)}, f32[2,8,66,1]{2,1,3,0:T(8,128)S(1)}, u32[]{:S(2)}, u32[]{:S(2)}) collective-permute-start(f32[2,8,66,1]{2,1,3,0:T(8,128)} %copy.195), channel_id=1, source_target_pairs={{0,1},{1,2},{2,3},{3,16},{16,17},{17,18},{18,19},{4,5},{5,6},{6,7}... | collective-permute-start | bytes 12680 | tf_op jit(solution)/shard_map/ppermute | solution.py:31
  111.6 1.9 %collective-permute-start.15 = (f32[2,8,66,1]{2,1,3,0:T(8,128)S(1)}, f32[2,8,66,1]{2,1,3,0:T(8,128)}, u32[]{:S(2)}, u32[]{:S(2)}) collective-permute-start(f32[2,8,66,1]{2,1,3,0:T(8,128)S(1)} %copy.197), channel_id=1, source_target_pairs={{1,0},{2,1},{3,2},{16,3},{17,16},{18,17},{19,18},{5,4},{6,5},{7,6}... | collective-permute-start | bytes 12680 | tf_op jit(solution)/shard_map/ppermute | solution.py:32
  114.8 2.0 %collective-permute-done.15 = f32[2,8,66,1]{2,1,3,0:T(8,128)} collective-permute-done((f32[2,8,66,1]{2,1,3,0:T(8,128)S(1)}, f32[2,8,66,1]{2,1,3,0:T(8,128)}, u32[]{:S(2)}, u32[]{:S(2)}) %collective-permute-start.15) | collective-permute-done | bytes 4256 | tf_op jit(solution)/shard_map/ppermute | solution.py:32
  117.9 1.8 fusion.23
  120.5 3.2 %collective-permute-start.20 = (f32[4,32,128]{2,1,0:T(8,128)S(1)}, f32[4,32,128]{2,1,0:T(8,128)S(1)}, u32[]{:S(2)}, u32[]{:S(2)}) collective-permute-start(f32[4,32,128]{2,1,0:T(8,128)S(1)} %get-tuple-element.129), channel_id=1, source_target_pairs={{0,4},{4,8},{8,12},{1,5},{5,9},{9,13},{2,6},{6,10},{10,14},{3,7},{... | collective-permute-start | bytes 196616 | tf_op jit(solution)/shard_map/ppermute | solution.py:31
  125.0 7.6 %while.10 = (s32[]{:T(128)}, f32[16,2,128]{2,0,1:T(8,128)S(1)}, s32[]{:T(128)}, s32[3,64]{1,0:T(4,128)S(1)}, s32[]{:T(128)}, /*index=5*/f32[48,5,128]{2,1,0:T(8,...) while((s32[]{:T(128)}, f32[16,2,128]{2,0,1:T(8,128)S(1)}, s32[]{:T(128)}, s32[3,64]{1,0:T(4,128)S(1)}, ...), condition=%wide.region_3.4_spmd, body=%wide.region_0.3_spmd.sunk | while | flops 15219718 | bytes 928223 | solution.py:151
  126.5 5.1 %multiply_reduce_fusion.4 = (f32[32,128]{1,0:T(8,128)S(1)}, f32[32,128]{1,0:T(8,128)S(1)}) fusion(f32[32,128]{1,0:T(8,128)S(1)} %bitcast.166, f32[32,128]{1,0:T(8,128)S(1)} %bitcast.171, f32[32,128]{1,0:T(8,128)S(1)} %bitcast.167, f32[32,128]{1,0:T(8,128)S(1)} %bitcast.172, f32[32,128]{1,0:T(8,128)S(1)} %bitcast.168, f32[32,128]{1,0:T(8,128)S(1)} %bitcast.173, ...), kind=kLoop, calls=%fused_computation.17.clone.1 | loop fusion | flops 13623296 | bytes 196608 | tf_op jit(solution)/shard_map/while/body/reduce_sum | solution.py:70
  132.7 4.7 %copy.203 = f32[4,128,128]{0,2,1:T(8,128)} copy(f32[4,128,128]{2,1,0:T(8,128)S(1)} %pad_maximum_fusion.38) | data formatting | bytes 524288 | tf_op jit(solution)/shard_map/concatenate | solution.py:33
  137.4 8.9 %gather_fusion.2 = f32[2048,4]{1,0:T(8,128)S(1)} fusion(f32[4,16384]{0,1:T(8,128)} %bitcast.154, s32[2048]{0:T(1024)S(1)} %copy-done.13), kind=kCustom, calls=%fused_computation.2 | custom fusion | bytes 73728 | tf_op jit(solution)/shard_map/jit(_take)/gather | solution.py:138
  146.8 1.4 copy.206
  148.2 1.4 copy.207
  149.6 3.4 %concatenate.178 = f32[38,2048]{0,1:T(8,128)S(1)} concatenate(f32[2,2048]{0,1:T(8,128)} %copy.206, f32[2,2048]{0,1:T(8,128)} %copy.207, f32[1,2048]{0,1:T(8,128)S(1)} %copy-done, f32[1,2048]{0,1:T(8,128)} %copy.209, f32[32,2048]{0,1:T(8,128)S(1)} %bitcast.155), dimensions={0} | concatenate | bytes 622592 | tf_op jit(solution)/shard_map/concatenate | solution.py:160
  153.1 2.8 %gather_fusion.3 = f32[1024,38]{1,0:T(8,128)S(1)} fusion(f32[38,2048]{0,1:T(8,128)S(1)} %concatenate.178, s32[1024]{0:T(1024)S(1)} %broadcast_clamp_fusion.1), kind=kCustom, calls=%fused_computation.3 | custom fusion | bytes 315392 | tf_op jit(solution)/shard_map/jit(_take)/gather | solution.py:165
  156.1 4.0 %collective-permute-start.22 = (f32[1,1,8,38,128]{4,2,3,1,0:T(8,128)S(1)}, f32[1,1,8,38,128]{4,2,3,1,0:T(8,128)S(1)}, u32[]{:S(2)}, u32[]{:S(2)}) collective-permute-start(f32[1,1,8,38,128]{4,2,3,1,0:T(8,128)S(1)} %select_bitcast_fusion), channel_id=1, source_target_pairs={{0,4},{4,8},{8,12},{1,5},{5,9},{9,13},{2,6},{6,10},{10,14},{3,7},{... | collective-permute-start | bytes 466952 | tf_op jit(solution)/shard_map/ppermute | solution.py:31
  162.3 3.8 %collective-permute-done.23 = f32[1,1,8,38,128]{4,2,3,1,0:T(8,128)S(1)} collective-permute-done((f32[1,1,8,38,128]{4,2,3,1,0:T(8,128)S(1)}, f32[1,1,8,38,128]{4,2,3,1,0:T(8,128)S(1)}, u32[]{:S(2)}, u32[]{:S(2)}) %collective-permute-start.23) | collective-permute-done | bytes 155680 | tf_op jit(solution)/shard_map/ppermute | solution.py:32
  166.2 4.4 %collective-permute-start.24 = (f32[3,1,8,38,128]{4,2,3,1,0:T(8,128)S(1)}, f32[3,1,8,38,128]{4,2,3,1,0:T(8,128)S(1)}, u32[]{:S(2)}, u32[]{:S(2)}) collective-permute-start(f32[3,1,8,38,128]{4,2,3,1,0:T(8,128)S(1)} %pad_maximum_fusion.37), channel_id=1, source_target_pairs={{0,1},{1,2},{2,3},{3,16},{16,17},{17,18},{18,19},{4,5},{5,6},{6,7}... | collective-permute-start | bytes 1400840 | tf_op jit(solution)/shard_map/ppermute | solution.py:31
  170.5 5.4 %collective-permute-start.25 = (f32[3,1,8,38,128]{4,2,3,1,0:T(8,128)S(1)}, f32[3,1,8,38,128]{4,2,3,1,0:T(8,128)S(1)}, u32[]{:S(2)}, u32[]{:S(2)}) collective-permute-start(f32[3,1,8,38,128]{4,2,3,1,0:T(8,128)S(1)} %pad_maximum_fusion.37), channel_id=1, source_target_pairs={{1,0},{2,1},{3,2},{16,3},{17,16},{18,17},{19,18},{5,4},{6,5},{7,6}... | collective-permute-start | bytes 1400840 | tf_op jit(solution)/shard_map/ppermute | solution.py:32
  177.5 12.2 %collective-permute-done.25 = f32[3,1,8,38,128]{4,2,3,1,0:T(8,128)S(1)} collective-permute-done((f32[3,1,8,38,128]{4,2,3,1,0:T(8,128)S(1)}, f32[3,1,8,38,128]{4,2,3,1,0:T(8,128)S(1)}, u32[]{:S(2)}, u32[]{:S(2)}) %collective-permute-start.25) | collective-permute-done | bytes 466976 | tf_op jit(solution)/shard_map/ppermute | solution.py:32
  (157 shorter events, 44.5 us)
Async XLA Ops:
  2.0 31.0 %collective-permute-start.16 = (f32[1,1,5,512]{3,2,1,0:T(8,128)}, f32[1,1,5,512]{3,2,1,0:T(8,128)}, u32[]{:S(2)}, u32[]{:S(2)}) collective-permute-start(f32[1,1,5,512]{3,2,1,0:T(8,128)} %fusion.68), channel_id=1, source_target_pairs={{0,4},{4,8},{8,12},{1,5},{5,9},{9,13},{2,6},{6,10},{10,14},{3,7},{... | collective-permute-start | bytes 30728 | tf_op jit(solution)/shard_map/ppermute | solution.py:31
  6.6 29.1 %collective-permute-start.17 = (f32[1,1,5,512]{3,2,1,0:T(8,128)}, f32[1,1,5,512]{3,2,1,0:T(8,128)}, u32[]{:S(2)}, u32[]{:S(2)}) collective-permute-start(f32[1,1,5,512]{3,2,1,0:T(8,128)} %fusion.68), channel_id=1, source_target_pairs={{4,0},{8,4},{12,8},{5,1},{9,5},{13,9},{6,2},{10,6},{14,10},{7,3},{... | collective-permute-start | bytes 30728 | tf_op jit(solution)/shard_map/ppermute | solution.py:32
  8.7 8.6 %copy-start.4 = (f32[2,64,128]{2,1,0:T(8,128)S(1)}, f32[2,64,128]{2,1,0:T(8,128)}, u32[]{:S(2)}) copy-start(f32[2,64,128]{2,1,0:T(8,128)} %param.16) | copy-start | bytes 196612
  10.1 7.2 %copy-start.19 = (s32[1,1,2048]{2,1,0:T(1,128)S(1)}, s32[1,1,2048]{2,1,0:T(1,128)}, u32[]{:S(2)}) copy-start(s32[1,1,2048]{2,1,0:T(1,128)} %param.23) | copy-start | bytes 24580
  10.1 8.4 %copy-start.18 = (s32[1,1,8,128]{3,2,1,0:T(8,128)S(1)}, s32[1,1,8,128]{3,2,1,0:T(8,128)}, u32[]{:S(2)}) copy-start(s32[1,1,8,128]{3,2,1,0:T(8,128)} %param.26) | copy-start | bytes 12292
  10.1 8.4 %copy-start.24 = (s32[1,1,8]{2,1,0:T(1,128)S(1)}, s32[1,1,8]{2,1,0:T(1,128)}, u32[]{:S(2)}) copy-start(s32[1,1,8]{2,1,0:T(1,128)} %param.27) | copy-start | bytes 100
  10.1 9.0 %copy-start.7 = (f32[1,1,2,2048]{3,2,1,0:T(2,128)S(1)}, f32[1,1,2,2048]{3,2,1,0:T(2,128)}, u32[]{:S(2)}) copy-start(f32[1,1,2,2048]{3,2,1,0:T(2,128)} %param.19) | copy-start | bytes 49156
  10.1 9.0 %copy-start.9 = (f32[1,1,2,2048]{3,2,1,0:T(2,128)S(1)}, f32[1,1,2,2048]{3,2,1,0:T(2,128)}, u32[]{:S(2)}) copy-start(f32[1,1,2,2048]{3,2,1,0:T(2,128)} %param.18) | copy-start | bytes 49156
  10.1 9.0 %copy-start.10 = (f32[1,1,2048]{2,1,0:T(1,128)S(1)}, f32[1,1,2048]{2,1,0:T(1,128)}, u32[]{:S(2)}) copy-start(f32[1,1,2048]{2,1,0:T(1,128)} %param.20) | copy-start | bytes 24580
  10.2 13.8 %collective-permute-start = (f32[2,8,1,128]{3,1,2,0:T(8,128)S(1)}, f32[2,8,1,128]{3,1,2,0:T(8,128)S(1)}, u32[]{:S(2)}, u32[]{:S(2)}) collective-permute-start(f32[2,8,1,128]{3,1,2,0:T(8,128)S(1)} %get-tuple-element.122), channel_id=1, source_target_pairs={{0,4},{4,8},{8,12},{1,5},{5,9},{9,13},{2,6},{6,10},{10,14},{3,7},{... | collective-permute-start | bytes 24584 | tf_op jit(solution)/shard_map/ppermute | solution.py:31
  14.3 9.7 %collective-permute-start.1 = (f32[2,8,1,128]{3,1,2,0:T(8,128)S(1)}, f32[2,8,1,128]{3,1,2,0:T(8,128)S(1)}, u32[]{:S(2)}, u32[]{:S(2)}) collective-permute-start(f32[2,8,1,128]{3,1,2,0:T(8,128)S(1)} %get-tuple-element.123), channel_id=1, source_target_pairs={{4,0},{8,4},{12,8},{5,1},{9,5},{13,9},{6,2},{10,6},{14,10},{7,3},{... | collective-permute-start | bytes 24584 | tf_op jit(solution)/shard_map/ppermute | solution.py:32
  15.6 6.7 %copy-start.23 = (s32[1,1,3,64]{3,1,2,0:T(1,128)S(1)}, s32[1,1,3,64]{3,1,2,0:T(1,128)}, u32[]{:S(2)}) copy-start(s32[1,1,3,64]{3,1,2,0:T(1,128)} %param.25) | copy-start | bytes 2308
  15.6 6.7 %copy-start.6 = (f32[1,1,32,2048]{3,2,1,0:T(8,128)S(1)}, f32[1,1,32,2048]{3,2,1,0:T(8,128)}, u32[]{:S(2)}) copy-start(f32[1,1,32,2048]{3,2,1,0:T(8,128)} %param.22) | copy-start | bytes 786436
  16.4 6.2 %copy-start.11 = (f32[1,1,2048]{2,1,0:T(1,128)S(1)}, f32[1,1,2048]{2,1,0:T(1,128)}, u32[]{:S(2)}) copy-start(f32[1,1,2048]{2,1,0:T(1,128)} %param.21) | copy-start | bytes 24580
  26.3 16.3 %collective-permute-start.2 = (f32[2,8,66,1]{2,1,3,0:T(8,128)}, f32[2,8,66,1]{2,1,3,0:T(8,128)S(1)}, u32[]{:S(2)}, u32[]{:S(2)}) collective-permute-start(f32[2,8,66,1]{2,1,3,0:T(8,128)} %copy.183), channel_id=1, source_target_pairs={{0,1},{1,2},{2,3},{3,16},{16,17},{17,18},{18,19},{4,5},{5,6},{6,7}... | collective-permute-start | bytes 12680 | tf_op jit(solution)/shard_map/ppermute | solution.py:31
  31.1 11.8 %collective-permute-start.3 = (f32[2,8,66,1]{2,1,3,0:T(8,128)S(1)}, f32[2,8,66,1]{2,1,3,0:T(8,128)S(1)}, u32[]{:S(2)}, u32[]{:S(2)}) collective-permute-start(f32[2,8,66,1]{2,1,3,0:T(8,128)S(1)} %copy.185), channel_id=1, source_target_pairs={{1,0},{2,1},{3,2},{16,3},{17,16},{18,17},{19,18},{5,4},{6,5},{7,6}... | collective-permute-start | bytes 12680 | tf_op jit(solution)/shard_map/ppermute | solution.py:32
  37.0 64.5 %collective-permute-start.18 = (f32[3,1,5,512]{3,1,2,0:T(1,128)}, f32[3,1,5,512]{3,1,2,0:T(1,128)}, u32[]{:S(2)}, u32[]{:S(2)}) collective-permute-start(f32[3,1,5,512]{3,1,2,0:T(1,128)} %copy_dynamic-update-slice_fusion), channel_id=1, source_target_pairs={{0,1},{1,2},{2,3},{3,16},{16,17},{17,18},{18,19},{4,5},{5,6},{6,7}... | collective-permute-start | bytes 92168 | tf_op jit(solution)/shard_map/ppermute | solution.py:31
  40.6 60.8 %collective-permute-start.19 = (f32[3,1,5,512]{3,1,2,0:T(1,128)}, f32[3,1,5,512]{3,1,2,0:T(1,128)}, u32[]{:S(2)}, u32[]{:S(2)}) collective-permute-start(f32[3,1,5,512]{3,1,2,0:T(1,128)} %copy_dynamic-update-slice_fusion), channel_id=1, source_target_pairs={{1,0},{2,1},{3,2},{16,3},{17,16},{18,17},{19,18},{5,4},{6,5},{7,6}... | collective-permute-start | bytes 92168 | tf_op jit(solution)/shard_map/ppermute | solution.py:32
  46.0 5.7 %collective-permute-start.4 = (f32[2,8,1,128]{3,1,2,0:T(8,128)S(1)}, f32[2,8,1,128]{3,1,2,0:T(8,128)S(1)}, u32[]{:S(2)}, u32[]{:S(2)}) collective-permute-start(f32[2,8,1,128]{3,1,2,0:T(8,128)S(1)} %get-tuple-element.118), channel_id=1, source_target_pairs={{0,4},{4,8},{8,12},{1,5},{5,9},{9,13},{2,6},{6,10},{10,14},{3,7},{... | collective-permute-start | bytes 24584 | tf_op jit(solution)/shard_map/ppermute | solution.py:31
  50.3 4.4 %collective-permute-start.5 = (f32[2,8,1,128]{3,1,2,0:T(8,128)S(1)}, f32[2,8,1,128]{3,1,2,0:T(8,128)S(1)}, u32[]{:S(2)}, u32[]{:S(2)}) collective-permute-start(f32[2,8,1,128]{3,1,2,0:T(8,128)S(1)} %get-tuple-element.119), channel_id=1, source_target_pairs={{4,0},{8,4},{12,8},{5,1},{9,5},{13,9},{6,2},{10,6},{14,10},{7,3},{... | collective-permute-start | bytes 24584 | tf_op jit(solution)/shard_map/ppermute | solution.py:32
  57.6 8.6 %collective-permute-start.6 = (f32[2,8,66,1]{2,1,3,0:T(8,128)}, f32[2,8,66,1]{2,1,3,0:T(8,128)}, u32[]{:S(2)}, u32[]{:S(2)}) collective-permute-start(f32[2,8,66,1]{2,1,3,0:T(8,128)} %copy.187), channel_id=1, source_target_pairs={{0,1},{1,2},{2,3},{3,16},{16,17},{17,18},{18,19},{4,5},{5,6},{6,7}... | collective-permute-start | bytes 12680 | tf_op jit(solution)/shard_map/ppermute | solution.py:31
  63.5 5.2 %collective-permute-start.7 = (f32[2,8,66,1]{2,1,3,0:T(8,128)}, f32[2,8,66,1]{2,1,3,0:T(8,128)S(1)}, u32[]{:S(2)}, u32[]{:S(2)}) collective-permute-start(f32[2,8,66,1]{2,1,3,0:T(8,128)} %copy.189), channel_id=1, source_target_pairs={{1,0},{2,1},{3,2},{16,3},{17,16},{18,17},{19,18},{5,4},{6,5},{7,6}... | collective-permute-start | bytes 12680 | tf_op jit(solution)/shard_map/ppermute | solution.py:32
  71.5 5.0 %collective-permute-start.8 = (f32[2,8,1,128]{3,1,2,0:T(8,128)S(1)}, f32[2,8,1,128]{3,1,2,0:T(8,128)S(1)}, u32[]{:S(2)}, u32[]{:S(2)}) collective-permute-start(f32[2,8,1,128]{3,1,2,0:T(8,128)S(1)} %get-tuple-element.114), channel_id=1, source_target_pairs={{0,4},{4,8},{8,12},{1,5},{5,9},{9,13},{2,6},{6,10},{10,14},{3,7},{... | collective-permute-start | bytes 24584 | tf_op jit(solution)/shard_map/ppermute | solution.py:31
  74.3 4.7 %collective-permute-start.9 = (f32[2,8,1,128]{3,1,2,0:T(8,128)S(1)}, f32[2,8,1,128]{3,1,2,0:T(8,128)S(1)}, u32[]{:S(2)}, u32[]{:S(2)}) collective-permute-start(f32[2,8,1,128]{3,1,2,0:T(8,128)S(1)} %get-tuple-element.115), channel_id=1, source_target_pairs={{4,0},{8,4},{12,8},{5,1},{9,5},{13,9},{6,2},{10,6},{14,10},{7,3},{... | collective-permute-start | bytes 24584 | tf_op jit(solution)/shard_map/ppermute | solution.py:32
  80.2 13.2 %copy-start.3 = (f32[2,7,64,128]{3,1,2,0:T(8,128)S(1)}, f32[2,7,64,128]{3,1,2,0:T(8,128)}, u32[]{:S(2)}) copy-start(f32[2,7,64,128]{3,1,2,0:T(8,128)} %fusion.33) | copy-start | bytes 1376260
  81.6 8.1 %collective-permute-start.10 = (f32[2,8,66,1]{2,1,3,0:T(8,128)S(1)}, f32[2,8,66,1]{2,1,3,0:T(8,128)S(1)}, u32[]{:S(2)}, u32[]{:S(2)}) collective-permute-start(f32[2,8,66,1]{2,1,3,0:T(8,128)S(1)} %copy.191), channel_id=1, source_target_pairs={{0,1},{1,2},{2,3},{3,16},{16,17},{17,18},{18,19},{4,5},{5,6},{6,7}... | collective-permute-start | bytes 12680 | tf_op jit(solution)/shard_map/ppermute | solution.py:31
  87.0 5.4 %collective-permute-start.11 = (f32[2,8,66,1]{2,1,3,0:T(8,128)S(1)}, f32[2,8,66,1]{2,1,3,0:T(8,128)S(1)}, u32[]{:S(2)}, u32[]{:S(2)}) collective-permute-start(f32[2,8,66,1]{2,1,3,0:T(8,128)S(1)} %copy.193), channel_id=1, source_target_pairs={{1,0},{2,1},{3,2},{16,3},{17,16},{18,17},{19,18},{5,4},{6,5},{7,6}... | collective-permute-start | bytes 12680 | tf_op jit(solution)/shard_map/ppermute | solution.py:32
  96.8 6.3 %collective-permute-start.12 = (f32[2,8,1,128]{3,1,2,0:T(8,128)S(1)}, f32[2,8,1,128]{3,1,2,0:T(8,128)S(1)}, u32[]{:S(2)}, u32[]{:S(2)}) collective-permute-start(f32[2,8,1,128]{3,1,2,0:T(8,128)S(1)} %get-tuple-element.110), channel_id=1, source_target_pairs={{0,4},{4,8},{8,12},{1,5},{5,9},{9,13},{2,6},{6,10},{10,14},{3,7},{... | collective-permute-start | bytes 24584 | tf_op jit(solution)/shard_map/ppermute | solution.py:31
  100.2 4.4 %collective-permute-start.13 = (f32[2,8,1,128]{3,1,2,0:T(8,128)S(1)}, f32[2,8,1,128]{3,1,2,0:T(8,128)S(1)}, u32[]{:S(2)}, u32[]{:S(2)}) collective-permute-start(f32[2,8,1,128]{3,1,2,0:T(8,128)S(1)} %get-tuple-element.111), channel_id=1, source_target_pairs={{4,0},{8,4},{12,8},{5,1},{9,5},{13,9},{6,2},{10,6},{14,10},{7,3},{... | collective-permute-start | bytes 24584 | tf_op jit(solution)/shard_map/ppermute | solution.py:32
  103.1 10.4 %copy-start.8 = (f32[16,5,128]{2,1,0:T(8,128)S(1)}, f32[16,5,128]{2,1,0:T(8,128)}, u32[]{:S(2)}) copy-start(f32[16,5,128]{2,1,0:T(8,128)} %maximum_bitcast_fusion) | copy-start | bytes 122884
  103.1 1.4 copy-start.16
  106.3 8.3 %collective-permute-start.14 = (f32[2,8,66,1]{2,1,3,0:T(8,128)}, f32[2,8,66,1]{2,1,3,0:T(8,128)S(1)}, u32[]{:S(2)}, u32[]{:S(2)}) collective-permute-start(f32[2,8,66,1]{2,1,3,0:T(8,128)} %copy.195), channel_id=1, source_target_pairs={{0,1},{1,2},{2,3},{3,16},{16,17},{17,18},{18,19},{4,5},{5,6},{6,7}... | collective-permute-start | bytes 12680 | tf_op jit(solution)/shard_map/ppermute | solution.py:31
  111.6 5.2 %collective-permute-start.15 = (f32[2,8,66,1]{2,1,3,0:T(8,128)S(1)}, f32[2,8,66,1]{2,1,3,0:T(8,128)}, u32[]{:S(2)}, u32[]{:S(2)}) collective-permute-start(f32[2,8,66,1]{2,1,3,0:T(8,128)S(1)} %copy.197), channel_id=1, source_target_pairs={{1,0},{2,1},{3,2},{16,3},{17,16},{18,17},{19,18},{5,4},{6,5},{7,6}... | collective-permute-start | bytes 12680 | tf_op jit(solution)/shard_map/ppermute | solution.py:32
  114.8 5.7 %copy-start.5 = (f32[2,64,128]{2,1,0:T(8,128)S(1)}, f32[2,64,128]{2,1,0:T(8,128)}, u32[]{:S(2)}) copy-start(f32[2,64,128]{2,1,0:T(8,128)} %param.16) | copy-start | bytes 196612
  119.7 0.8 copy-start.1
  120.5 12.1 %collective-permute-start.20 = (f32[4,32,128]{2,1,0:T(8,128)S(1)}, f32[4,32,128]{2,1,0:T(8,128)S(1)}, u32[]{:S(2)}, u32[]{:S(2)}) collective-permute-start(f32[4,32,128]{2,1,0:T(8,128)S(1)} %get-tuple-element.129), channel_id=1, source_target_pairs={{0,4},{4,8},{8,12},{1,5},{5,9},{9,13},{2,6},{6,10},{10,14},{3,7},{... | collective-permute-start | bytes 196616 | tf_op jit(solution)/shard_map/ppermute | solution.py:31
  123.7 8.9 %collective-permute-start.21 = (f32[4,32,128]{2,1,0:T(8,128)S(1)}, f32[4,32,128]{2,1,0:T(8,128)S(1)}, u32[]{:S(2)}, u32[]{:S(2)}) collective-permute-start(f32[4,32,128]{2,1,0:T(8,128)S(1)} %get-tuple-element.130), channel_id=1, source_target_pairs={{4,0},{8,4},{12,8},{5,1},{9,5},{13,9},{6,2},{10,6},{14,10},{7,3},{... | collective-permute-start | bytes 196616 | tf_op jit(solution)/shard_map/ppermute | solution.py:32
  132.7 4.7 %copy-start.13 = (s32[2048]{0:T(1024)S(1)}, s32[2048]{0:T(1024)}, u32[]{:S(2)}) copy-start(s32[2048]{0:T(1024)} %broadcast_clamp_fusion) | copy-start | bytes 24580
  132.7 14.0 %copy-start.20 = (pred[2048]{0:T(1024)(128)(4,1)S(1)}, pred[2048]{0:T(1024)(128)(4,1)}, u32[]{:S(2)}) copy-start(pred[2048]{0:T(1024)(128)(4,1)} %compare_and_fusion) | copy-start | bytes 6148
  132.7 14.1 %copy-start.12 = (f32[1,1,2048]{2,1,0:T(1,128)S(1)}, f32[1,1,2048]{2,1,0:T(1,128)}, u32[]{:S(2)}) copy-start(f32[1,1,2048]{2,1,0:T(1,128)} %param.21) | copy-start | bytes 24580
  137.4 12.2 %copy-start = (f32[1,2048]{0,1:T(8,128)S(1)}, f32[1,2048]{0,1:T(8,128)}, u32[]{:S(2)}) copy-start(f32[1,2048]{0,1:T(8,128)} %copy.208) | copy-start | bytes 24580
  153.0 3.1 %copy-start.21 = (pred[8,128]{1,0:T(8,128)(4,1)S(1)}, pred[8,128]{1,0:T(8,128)(4,1)}, u32[]{:S(2)}) copy-start(pred[8,128]{1,0:T(8,128)(4,1)} %get-tuple-element.133) | copy-start | bytes 3076
  153.1 3.1 %copy-start.22 = (pred[8,128]{1,0:T(8,128)(4,1)S(1)}, pred[8,128]{1,0:T(8,128)(4,1)}, u32[]{:S(2)}) copy-start(pred[8,128]{1,0:T(8,128)(4,1)} %get-tuple-element.134) | copy-start | bytes 3076
  153.1 22.9 %copy-start.2 = (f32[2,8,64,128]{3,1,2,0:T(8,128)S(1)}, f32[2,8,64,128]{3,1,2,0:T(8,128)}, u32[]{:S(2)}) copy-start(f32[2,8,64,128]{3,1,2,0:T(8,128)} %copy-done.1) | copy-start | bytes 1572868
  156.1 6.2 %collective-permute-start.22 = (f32[1,1,8,38,128]{4,2,3,1,0:T(8,128)S(1)}, f32[1,1,8,38,128]{4,2,3,1,0:T(8,128)S(1)}, u32[]{:S(2)}, u32[]{:S(2)}) collective-permute-start(f32[1,1,8,38,128]{4,2,3,1,0:T(8,128)S(1)} %select_bitcast_fusion), channel_id=1, source_target_pairs={{0,4},{4,8},{8,12},{1,5},{5,9},{9,13},{2,6},{6,10},{10,14},{3,7},{... | collective-permute-start | bytes 466952 | tf_op jit(solution)/shard_map/ppermute | solution.py:31
  160.2 6.0 %collective-permute-start.23 = (f32[1,1,8,38,128]{4,2,3,1,0:T(8,128)S(1)}, f32[1,1,8,38,128]{4,2,3,1,0:T(8,128)S(1)}, u32[]{:S(2)}, u32[]{:S(2)}) collective-permute-start(f32[1,1,8,38,128]{4,2,3,1,0:T(8,128)S(1)} %select_bitcast_fusion), channel_id=1, source_target_pairs={{4,0},{8,4},{12,8},{5,1},{9,5},{13,9},{6,2},{10,6},{14,10},{7,3},{... | collective-permute-start | bytes 466952 | tf_op jit(solution)/shard_map/ppermute | solution.py:32
  166.2 11.3 %collective-permute-start.24 = (f32[3,1,8,38,128]{4,2,3,1,0:T(8,128)S(1)}, f32[3,1,8,38,128]{4,2,3,1,0:T(8,128)S(1)}, u32[]{:S(2)}, u32[]{:S(2)}) collective-permute-start(f32[3,1,8,38,128]{4,2,3,1,0:T(8,128)S(1)} %pad_maximum_fusion.37), channel_id=1, source_target_pairs={{0,1},{1,2},{2,3},{3,16},{16,17},{17,18},{18,19},{4,5},{5,6},{6,7}... | collective-permute-start | bytes 1400840 | tf_op jit(solution)/shard_map/ppermute | solution.py:31
  170.5 19.2 %collective-permute-start.25 = (f32[3,1,8,38,128]{4,2,3,1,0:T(8,128)S(1)}, f32[3,1,8,38,128]{4,2,3,1,0:T(8,128)S(1)}, u32[]{:S(2)}, u32[]{:S(2)}) collective-permute-start(f32[3,1,8,38,128]{4,2,3,1,0:T(8,128)S(1)} %pad_maximum_fusion.37), channel_id=1, source_target_pairs={{1,0},{2,1},{3,2},{16,3},{17,16},{18,17},{19,18},{5,4},{6,5},{7,6}... | collective-permute-start | bytes 1400840 | tf_op jit(solution)/shard_map/ppermute | solution.py:32
  (3 other events, 1.8 us)
where the time goes:
time: 193 us; the launch traced here: 191 us
  starting transfers between devices  77.1 us (40%)
  local copies, waits for them, and re-layouts  55 us (28%)
  other arithmetic  28.1 us (15%)
  waiting for transfers between devices  28.1 us (15%)
  between operations  2.08 us (1%)
    ppermute x13, starting transfers between devices, with_halo(): before = lax.ppermute(last, axis, up)  53.1 us
    ppermute x13, waiting for transfers between devices, with_halo(): after = lax.ppermute(leading, axis, down)  27.3 us
    ppermute x13, starting transfers between devices, with_halo(): after = lax.ppermute(leading, axis, down)  24.1 us
    gather x2, local copies, waits for them, and re-layouts, shards(): jnp.take(near.reshape(4, -1), cells - first_row * cols_here, axis=1)  9.26 us
    slice x13, local copies, waits for them, and re-layouts, with_halo(): last = lax.slice_in_dim(array, length - width, length, axis=dim)  7.6 us
    mul x4, other arithmetic, ocean_substep(): return (flow + horizontal * lap + vert + turning + surface) * wet[None]  7.26 us
    unnamed x55, local copies, waits for them, and re-layouts  6.56 us
    concatenate x3, local copies, waits for them, and re-layouts, with_halo(): array = jnp.concatenate([before, array, after], axis=dim)  6.05 us
  transfers between devices with their start and end apart: 26, of which 9 were waited for; matrix products, arithmetic and copies ran while one was open for 27% of the time, Pallas kernels for 0%

commit v1 on v0

v1 whole, which is shorter than its diff:
```python
import functools
import math

import jax
import jax.numpy as jnp
from jax import lax
from jax.experimental import pallas as pl
from jax.experimental.pallas import tpu as pltpu
from jax.sharding import PartitionSpec as P

OSTEPS = 4
GHOST = 4
SOFTEN = 0.1
STIFFNESS = 0.1
DAMPING = 0.05
VERT_MIX = 0.15
CORIOLIS = 0.1
SURFACE_GAIN = 0.25
WATER_DRAG = 0.1
AIR_GAIN = 0.2
ICE_STEP = 0.5
PLACES = (0, 1, 2, 3, 5, 6, 7, 8)
UP, LEFT, RIGHT, DOWN = 1, 3, 4, 6
MESH = pl.DeviceIdType.MESH
f32 = jnp.float32
UNROLL = 2


def lane_gather(values, lanes):
    return jnp.take_along_axis(values, lanes, axis=1, mode="promise_in_bounds")


def iota(shape, dim):
    return lax.broadcasted_iota(jnp.int32, shape, dim)


def kernel(
    ocean, wind, counts, pos, vel, rad, mass, poly, cells, ccount, clist, clist_v, mindex, mcount,
    ocean_out, floe_out, arrive_out,
    flow, cnt, wnd, halo_o, halo_c, pack, side, corner, edge72, own, gh, cols, forces,
    surf, late_s, early_s, early_r, next_s, next_r,
    sem_s, sem_r,
):
    levels, rows, width = ocean.shape[1], ocean.shape[2], ocean.shape[3]
    floes = pos.shape[1]
    blocks = floes // 128
    ext = rows + 8
    margin = rows // 2
    slots = clist.shape[1]
    n_gy = lax.axis_size("gy")
    n_rows, n_cols = lax.axis_size("gx"), lax.axis_size("sec") * n_gy
    row = lax.axis_index("gx")
    col = lax.axis_index("sec") * n_gy + lax.axis_index("gy")

    there, ids = [], []
    for way in range(8):
        dr, dc = PLACES[way] // 3 - 1, PLACES[way] % 3 - 1
        r, c = row + dr, col + dc
        there.append((r >= 0) & (r < n_rows) & (c >= 0) & (c < n_cols))
        ids.append((c // n_gy, r, c % n_gy))

    def copy(src, dst, number, way):
        return pltpu.make_async_remote_copy(
            src_ref=src, dst_ref=dst, send_sem=sem_s.at[number], recv_sem=sem_r.at[number],
            device_id=ids[way], device_id_type=MESH,
        )

    for ref in (halo_o, halo_c, side, corner, gh, early_r, next_r):
        ref[...] = jnp.zeros_like(ref)
    surf[:, 0:margin] = jnp.zeros((4, margin, width), f32)
    surf[:, margin + rows :] = jnp.zeros((4, margin, width), f32)

    barrier = pltpu.get_barrier_semaphore()
    for way in range(8):
        @pl.when(there[way])
        def _():
            pl.semaphore_signal(barrier, inc=1, device_id=ids[way], device_id_type=MESH)

    for b in range(blocks):
        at = slice(128 * b, 128 * b + 128)
        own[b, 0:2] = pos[:, at]
        own[b, 2:4] = vel[:, at]
        own[b, 4:5] = rad[:, at]
        own[b, 5:8] = jnp.zeros((3, 128), f32)
    lane = iota((rows, width), 1)
    group = lane // 8
    pack_flow = jnp.zeros((rows, width), f32)
    for c in range(2):
        for k in range(levels):
            n = c * levels + k
            pack_flow = jnp.where(group == n, pltpu.roll(ocean[c, k], (8 * n + 4) % width, 1), pack_flow)
    pack[0] = pack_flow
    countf = counts[...].astype(f32)
    aux = jnp.zeros((rows, width), f32)
    for c in range(2):
        n = c * levels
        aux = jnp.where(group == n, pltpu.roll(wind[c], (8 * n + 4) % width, 1), aux)
        aux = jnp.where(group == n + 1, pltpu.roll(countf, (8 * n + 12) % width, 1), aux)
    pack[1] = aux

    pl.semaphore_wait(barrier, sum(t.astype(jnp.int32) for t in there))

    halo = []
    strips = []
    for way in range(8):
        dr, dc = PLACES[way] // 3 - 1, PLACES[way] % 3 - 1
        first = 0 if dr < 0 else rows - 8
        if dr == 0:
            halo.append((way, copy(pack, side.at[(dc + 1) // 2], way, way)))
        else:
            part = pl.ds(first, 8)
            d = (dr + 1) // 2
            halo.append((way, copy(pack.at[:, part], corner.at[d, dc + 1], way, way)))
            if dc == 0:
                halo.append((way, copy(ocean.at[:, :, part], halo_o.at[d], 8 + d, way)))
                halo.append((way, copy(counts.at[part], halo_c.at[d], 10 + d, way)))
                src = pl.ds(0 if dr < 0 else rows - margin, margin)
                dst = pl.ds(rows + margin if dr < 0 else 0, margin)
                halo.append((way, copy(wind.at[:, src], surf.at[2:4, dst], 12 + d, way)))
                strips.append((way, copy(late_s.at[:, src], surf.at[0:2, dst], 14 + d, way)))
    records = [(w, copy(own.at[0:GHOST], gh.at[pl.ds((7 - w) * GHOST, GHOST)], 16 + w, w)) for w in range(8)]
    early = [(w, copy(early_s.at[w], early_r.at[w], 24 + w, w)) for w in range(8)]
    late = [(w, copy(next_s.at[w], next_r.at[w], 32 + w, w)) for w in range(8)]

    def start(copies):
        for way, c in copies:
            pl.when(there[way])(c.start)

    def landed(copies):
        for way, c in copies:
            pl.when(there[7 - way])(c.wait_recv)

    def sent(copies):
        for way, c in copies:
            pl.when(there[way])(c.wait_send)

    start(halo)
    start(records)

    lane8 = iota((8, 128), 1)

    def gather_early(w, carry):
        index = jnp.broadcast_to(mindex[pl.ds(w, 1)], (8, 128))
        block, lanes = index // 128, index % 128
        valid = lane8 < mcount[0, w]
        groups = [jnp.zeros((8, 128), f32) for _ in range(5)]
        for b in range(blocks):
            at = slice(128 * b, 128 * b + 128)
            hit = block == b
            for g in range(4):
                groups[g] = jnp.where(hit, lane_gather(poly[8 * g : 8 * g + 8, at], lanes), groups[g])
            rm = jnp.concatenate([rad[:, at], mass[:, at], jnp.zeros((6, 128), f32)], axis=0)
            groups[4] = jnp.where(hit, lane_gather(rm, lanes), groups[4])
        for g in range(5):
            early_s[w, 8 * g : 8 * g + 8] = jnp.where(valid, groups[g], 0.0)
        return carry

    lax.fori_loop(0, 8, gather_early, 0)
    start(early)

    def own_cols(b, carry):
        cols[b] = own[b].T
        return carry

    lax.fori_loop(0, blocks, own_cols, 0)

    landed(halo)
    sub8 = iota((8, width), 0)
    cnt[0:rows] = countf
    cnt[rows:] = jnp.where(sub8 < 4, halo_c[0], halo_c[1]).astype(f32)
    for c in range(2):
        wnd[c, 0:rows] = SURFACE_GAIN * wind[c]
        below, above = surf[2 + c, margin + rows : margin + rows + 8], surf[2 + c, margin - 8 : margin]
        wnd[c, rows:] = SURFACE_GAIN * jnp.where(sub8 < 4, below, above)
        surf[2 + c, margin : margin + rows] = wind[c]

    def fill(k, carry):
        wet = (cnt[...] > k.astype(f32)).astype(f32)
        for c in range(2):
            flow[c, k, 0:rows] = ocean[c, k] * wet[0:rows]
            flow[c, k, rows:] = jnp.where(sub8 < 4, halo_o[0, c, k], halo_o[1, c, k]) * wet[rows:]
        return carry

    lax.fori_loop(0, levels, fill, 0)

    lane72 = iota((ext, width), 1)
    inner = (lane72 % 8) < 4
    level72 = (lane72 // 8) % levels
    level_f = level72.astype(f32)

    def joined(part):
        return [
            jnp.concatenate([mid, jnp.where(sub8 < 4, corner[0, dc, part], corner[1, dc, part])], axis=0)
            for mid, dc in ((side[1, part], 2), (pack[part], 1), (side[0, part], 0))
        ]

    packed_aux, packed_flow = joined(1), joined(0)
    steer = []
    for which in range(2):
        mixed = [jnp.where(inner, p[which], p[which + 1]) for p in (packed_flow, packed_aux)]
        deep = jnp.where(level72 == 1, mixed[1], 0.0)
        for shift in (8, 16, 32):
            deep = deep + pltpu.roll(deep, shift, 1)
        wet = (deep > level_f).astype(f32)
        edge72[which, 0] = mixed[0] * wet
        edge72[which, 1] = wet
        edge72[which, 2] = jnp.where(level72 == 0, SURFACE_GAIN * mixed[1], 0.0)

    def substep(step, carry):
        def level(k, fluxes):
            after = jnp.minimum(k + 1, levels - 1)
            deep = cnt[...]
            wet = (deep > k.astype(f32)).astype(f32)
            wet_after = (deep > after.astype(f32)).astype(f32)
            h = 0.15 - 0.05 * k.astype(f32) / levels
            here = [flow[0, k], flow[1, k]]
            surface_on = jnp.where(k == 0, 1.0, 0.0)
            new_fluxes = []
            for c in range(2):
                x = here[c]
                at = 64 * c + 8 * k
                before = pltpu.roll(edge72[0, 0], 125 - at + jnp.where(at > 125, width, 0), 1)
                behind = pltpu.roll(edge72[1, 0], 123 - at, 1)
                left = jnp.where(lane72 == 0, before, pltpu.roll(x, 1, 1))
                right = jnp.where(lane72 == width - 1, behind, pltpu.roll(x, width - 1, 1))
                lap = pltpu.roll(x, 1, 0) + pltpu.roll(x, ext - 1, 0) + left + right - 4.0 * x
                flux = VERT_MIX * (flow[c, after] - x) * wet_after
                turn = CORIOLIS * here[1] if c == 0 else -CORIOLIS * here[0]
                new = x + h * lap + (flux - fluxes[c]) + turn + surface_on * wnd[c]
                flow[c, k] = new * wet
                new_fluxes.append(flux)
            return tuple(new_fluxes)

        nothing = jnp.zeros((ext, width), f32)
        lax.fori_loop(0, levels, level, (nothing, nothing))
        hp = 0.15 - 0.05 * level_f / levels
        turn_by = jnp.where(lane72 < 64, CORIOLIS, -CORIOLIS)
        for which in range(2):
            x, wet = edge72[which, 0], edge72[which, 1]
            lap = (
                pltpu.roll(x, 1, 0) + pltpu.roll(x, ext - 1, 0)
                + pltpu.roll(x, 1, 1) + pltpu.roll(x, width - 1, 1) - 4.0 * x
            )
            flux = VERT_MIX * (pltpu.roll(x, width - 8, 1) - x) * pltpu.roll(wet, width - 8, 1)
            flux = jnp.where(level72 < levels - 1, flux, 0.0)
            turn = turn_by * pltpu.roll(x, 64, 1)
            new = x + hp * lap + (flux - pltpu.roll(flux, 8, 1)) + turn + edge72[which, 2]
            edge72[which, 0] = new * wet
        return carry

    lax.fori_loop(0, OSTEPS, substep, 0)

    for c in range(2):
        late_s[c] = flow[c, 0, 0:rows]
    start(strips)
    for c in range(2):
        surf[c, margin : margin + rows] = late_s[c]

    def write(k, carry):
        for c in range(2):
            ocean_out[c, k] = flow[c, k, 0:rows]
        return carry

    lax.fori_loop(0, levels, write, 0)

    landed(records)

    def ghost_cols(b, carry):
        cols[blocks + b] = gh[b].T
        return carry

    lax.fori_loop(0, 8 * GHOST, ghost_cols, 0)

    def contact(t, carry):
        a, s, c = clist[0, t], clist[1, t], clist[2, t]
        neighbour = s - (s > 4).astype(jnp.int32)
        partner = jnp.where(s == 4, c, blocks + neighbour * GHOST + c)
        partner = jnp.clip(partner, 0, blocks + 8 * GHOST - 1)
        mine = own[a]
        other = cols[partner]
        step = 16
        xi, yi, ui, vi, ri = [jnp.broadcast_to(mine[f : f + 1], (step, 128)) for f in range(5)]
        sx = jnp.zeros((step, 128), f32)
        sy = jnp.zeros((step, 128), f32)
        for q in range(0, 128, step):
            xj, yj, uj, vj, rj = [
                jnp.broadcast_to(other[q : q + step, f : f + 1], (step, 128)) for f in range(5)
            ]
            dx, dy = xi - xj, yi - yj
            square = dx * dx + dy * dy + SOFTEN * SOFTEN
            inverse = lax.rsqrt(square)
            reach = ri + rj
            overlap = jnp.maximum(reach - square * inverse, 0.0)
            reduced = ri * rj / reach
            closing = ((ui - uj) * dx + (vi - vj) * dy) * inverse
            m = overlap * reduced * (STIFFNESS - DAMPING * closing) * inverse
            sx = sx + m * dx
            sy = sy + m * dy
        forces[0, pl.ds(t, 1)] = jnp.sum(sx, axis=0, keepdims=True)
        forces[1, pl.ds(t, 1)] = jnp.sum(sy, axis=0, keepdims=True)
        return carry

    lax.fori_loop(0, slots, contact, 0, unroll=UNROLL)
    takes = (iota((blocks, slots), 0) == clist_v[0:1]) & (iota((blocks, slots), 1) < ccount[0, 0])
    takes = takes.astype(f32)
    push = [
        jnp.dot(takes, forces[c], precision=lax.Precision.HIGHEST, preferred_element_type=f32)
        for c in range(2)
    ]

    landed(strips)
    pieces = []
    for n in range(4):
        turned = surf[n].T
        high = turned.astype(jnp.bfloat16)
        low = (turned - high.astype(f32)).astype(jnp.bfloat16)
        pieces.append(jnp.concatenate([high, low], axis=1))
    table = jnp.concatenate(pieces, axis=0)
    first_cell = (row * rows - margin) * width
    sub = iota((2 * rows, 128), 0)
    columns = iota((width, 128), 0)
    for b in range(blocks):
        at = slice(128 * b, 128 * b + 128)
        q = cells[:, at] - first_cell
        hit_row = (sub == q // width).astype(f32).astype(jnp.bfloat16)
        found = jnp.dot(table, jnp.concatenate([hit_row, hit_row], axis=0), preferred_element_type=f32)
        hit_col = columns == q % width
        su, sv, wx, wy = [
            jnp.sum(jnp.where(hit_col, found[width * n : width * n + width], 0.0), axis=0, keepdims=True)
            for n in range(4)
        ]
        r = rad[:, at]
        u, v = vel[0:1, at], vel[1:2, at]
        area = math.pi * r * r
        ru, rv = su - u, sv - v
        speed = jnp.sqrt(ru * ru + rv * rv)
        fx = push[0][b : b + 1] + area * (WATER_DRAG * speed * ru + AIR_GAIN * wx)
        fy = push[1][b : b + 1] + area * (WATER_DRAG * speed * rv + AIR_GAIN * wy)
        per_mass = ICE_STEP / mass[:, at]
        nu, nv = u + fx * per_mass, v + fy * per_mass
        floe_out[0:1, at] = pos[0:1, at] + ICE_STEP * nu
        floe_out[1:2, at] = pos[1:2, at] + ICE_STEP * nv
        floe_out[2:3, at] = nu
        floe_out[3:4, at] = nv

    def gather_late(w, carry):
        index = jnp.broadcast_to(mindex[pl.ds(w, 1)], (8, 128))
        block, lanes = index // 128, index % 128
        total = jnp.zeros((8, 128), f32)
        for b in range(blocks):
            values = floe_out[:, 128 * b : 128 * b + 128]
            values = jnp.concatenate([values, values], axis=0)
            total = jnp.where(block == b, lane_gather(values, lanes), total)
        next_s[w] = jnp.where(lane8 < mcount[0, w], total, 0.0)
        return carry

    lax.fori_loop(0, 8, gather_late, 0)
    start(late)
    landed(early)
    for w in range(8):
        arrive_out[w, 6:38] = early_r[w, 0:32]
        arrive_out[w, 4:6] = early_r[w, 32:34]
    landed(late)
    for w in range(8):
        arrive_out[w, 0:4] = next_r[w, 0:4]
    for copies in (halo, records, early, strips, late):
        sent(copies)


def shards(
    ocean_velocity, wind_stress, level_counts, floe_position, floe_velocity, floe_radius, floe_mass,
    floe_polygon, remap_cells, contact_count, contact_list, move_index, move_count,
):
    levels, rows, width = ocean_velocity.shape[1:]
    floes = floe_position.shape[-1]
    blocks = floes // 128
    slots = contact_list.shape[-1]
    ext = rows + 8
    lists = contact_list[0, 0]
    vmem = pl.BlockSpec(memory_space=pltpu.VMEM)
    smem = pl.BlockSpec(memory_space=pltpu.SMEM)
    fields = 2 + floe_polygon.shape[2] + 4
    flow, floe, arrivals = pl.pallas_call(
        kernel,
        out_shape=(
            jax.ShapeDtypeStruct(ocean_velocity.shape, f32),
            jax.ShapeDtypeStruct((4, floes), f32),
            jax.ShapeDtypeStruct((8, fields, 128), f32),
        ),
        in_specs=[vmem] * 9 + [smem, smem, vmem, vmem, smem],
        out_specs=(vmem, vmem, vmem),
        scratch_shapes=[
            pltpu.VMEM((2, levels, ext, width), f32),
            pltpu.VMEM((ext, width), f32),
            pltpu.VMEM((2, ext, width), f32),
            pltpu.VMEM((2, 2, levels, 8, width), f32),
            pltpu.VMEM((2, 8, width), jnp.int32),
            pltpu.VMEM((2, rows, width), f32),
            pltpu.VMEM((2, 2, rows, width), f32),
            pltpu.VMEM((2, 3, 2, 8, width), f32),
            pltpu.VMEM((2, 3, ext, width), f32),
            pltpu.VMEM((blocks, 8, 128), f32),
            pltpu.VMEM((8 * GHOST, 8, 128), f32),
            pltpu.VMEM((blocks + 8 * GHOST, 128, 8), f32),
            pltpu.VMEM((2, slots, 128), f32),
            pltpu.VMEM((4, 2 * rows, width), f32),
            pltpu.VMEM((2, rows, width), f32),
            pltpu.VMEM((8, 40, 128), f32),
            pltpu.VMEM((8, 40, 128), f32),
            pltpu.VMEM((8, 8, 128), f32),
            pltpu.VMEM((8, 8, 128), f32),
            pltpu.SemaphoreType.DMA((40,)),
            pltpu.SemaphoreType.DMA((40,)),
        ],
        compiler_params=pltpu.CompilerParams(
            collective_id=0, has_side_effects=True, vmem_limit_bytes=40 * 1024 * 1024
        ),
    )(
        ocean_velocity, wind_stress, level_counts, floe_position[0, 0], floe_velocity[0, 0],
        floe_radius[0], floe_mass[0], floe_polygon[0, 0], remap_cells[0], contact_count,
        lists, lists, move_index[0, 0], move_count[0],
    )
    return (flow, floe[None, None], arrivals[None, None])


def solution(mesh):
    tile = P("gx", ("sec", "gy"))
    return jax.shard_map(
        shards,
        mesh=mesh,
        in_specs=(
            P(None, None, "gx", ("sec", "gy")),
            P(None, "gx", ("sec", "gy")),
            tile, tile, tile, tile, tile, tile, tile, tile, tile, tile, tile,
        ),
        out_specs=(P(None, None, "gx", ("sec", "gy")), tile, tile),
        check_vma=False,
    )
```

time: 193 us -> 49 us (0.25)
  starting transfers between devices: 77.1 us -> 0 us
  local copies, waits for them, and re-layouts: 55 us -> 9.84 us
  Pallas kernels: 0 us -> 37.2 us
  other arithmetic: 28.1 us -> 0 us
  waiting for transfers between devices: 28.1 us -> 0 us
    ppermute x26 -> x0, starting transfers between devices: 77.1 us -> none  [the longest x13 53.1 us: with_halo(): before = lax.ppermute(last, axis, up)]
    pallas_call x0 -> x1, Pallas kernels: none -> 37.2 us  [shards(): pl.pallas_call(kernel, out_shape=(jax.ShapeDtypeStruct(ocean_velocity.sha...]
    ppermute x26 -> x0, waiting for transfers between devices: 28.1 us -> none  [the longest x13 27.3 us: with_halo(): after = lax.ppermute(leading, axis, down)]
    mul x16 -> x0, other arithmetic: 14.3 us -> none  [the longest x4 7.26 us: ocean_substep(): return (flow + horizontal * lap + vert + turning + surface) * wet[None]]
    gather x6 -> x0, local copies, waits for them, and re-layouts: 13.4 us -> none  [the longest x2 9.26 us: shards(): jnp.take(near.reshape(4, -1), cells - first_row * cols_here, axis=1)]
    slice x21 -> x0, local copies, waits for them, and re-layouts: 10.5 us -> none  [the longest x13 7.6 us: with_halo(): last = lax.slice_in_dim(array, length - width, length, axis=dim)]
    concatenate x4 -> x0, local copies, waits for them, and re-layouts: 9.5 us -> none  [the longest x3 6.05 us: with_halo(): array = jnp.concatenate([before, array, after], axis=dim)]
    ppermute x8 -> x0, local copies, waits for them, and re-layouts: 7.77 us -> none  [the longest x4 4.28 us: with_halo(): after = lax.ppermute(leading, axis, down)]
  transfers between devices with their start and end apart: 26 -> 0, of which waited for: 9 -> 0; matrix products, arithmetic and copies ran while one was open for 27% -> 0% of each run, Pallas kernels for 0% -> 0%
where the time goes in v1:
time: 49 us; the launch traced here: 48.4 us
  Pallas kernels  37.2 us (76%)
  local copies, waits for them, and re-layouts  9.84 us (20%)
  between operations  1.33 us (3%)
    pallas_call x1, Pallas kernels, shards(): pl.pallas_call(kernel, out_shape=(jax.ShapeDtypeStruct(ocean_velocity.sha...  37.2 us
    unnamed x26, local copies, waits for them, and re-layouts  9.84 us

profile of v1, /device:TPU:1, one launch (start us, length us, event | category | flops | bytes accessed | tf_op | source)
XLA Modules:
  0.0 48.4 jit_solution(4341620328373811601)
XLA Ops:
  0.6 0.0 copy-start.4
  1.3 0.0 copy-start.9
  1.3 0.7 %copy.19 = s32[1,1,3,64]{3,2,1,0:T(4,128)S(1)} copy(s32[1,1,3,64]{3,1,2,0:T(1,128)} %param.23) | data formatting | bytes 1536
  2.0 0.0 copy-start.10
  2.0 0.0 copy-done.4
  2.0 0.0 copy-done.9
  2.0 0.6 %copy-done.10 = s32[1,1,8]{2,1,0:T(1,128)S(1)} copy-done((s32[1,1,8]{2,1,0:T(1,128)S(1)}, s32[1,1,8]{2,1,0:T(1,128)}, u32[]{:S(2)}) %copy-start.10) | copy-done | bytes 56
  2.7 0.0 copy-start
  2.7 1.0 %copy-done = f32[2,8,64,128]{3,2,1,0:T(8,128)S(1)} copy-done((f32[2,8,64,128]{3,2,1,0:T(8,128)S(1)}, f32[2,8,64,128]{3,2,1,0:T(8,128)}, u32[]{:S(2)}) %copy-start) | copy-done | bytes 524312
  3.7 0.0 copy-start.1
  3.7 0.9 %copy-done.1 = f32[1,1,32,2048]{3,2,1,0:T(8,128)S(1)} copy-done((f32[1,1,32,2048]{3,2,1,0:T(8,128)S(1)}, f32[1,1,32,2048]{3,2,1,0:T(8,128)}, u32[]{:S(2)}) %copy-start.1) | copy-done | bytes 262168
  4.6 0.0 copy-start.2
  4.6 0.8 %copy-done.2 = f32[2,64,128]{2,1,0:T(8,128)S(1)} copy-done((f32[2,64,128]{2,1,0:T(8,128)S(1)}, f32[2,64,128]{2,1,0:T(8,128)}, u32[]{:S(2)}) %copy-start.2) | copy-done | bytes 65560
  5.5 0.0 copy-start.3
  5.5 0.8 %copy-done.3 = s32[64,128]{1,0:T(8,128)S(1)} copy-done((s32[64,128]{1,0:T(8,128)S(1)}, s32[64,128]{1,0:T(8,128)}, u32[]{:S(2)}) %copy-start.3) | copy-done | bytes 32792
  6.2 0.0 copy-start.5
  6.2 0.7 %copy-done.5 = f32[1,1,2,2048]{3,2,1,0:T(2,128)S(1)} copy-done((f32[1,1,2,2048]{3,2,1,0:T(2,128)S(1)}, f32[1,1,2,2048]{3,2,1,0:T(2,128)}, u32[]{:S(2)}) %copy-start.5) | copy-done | bytes 16408
  7.0 0.0 copy-start.6
  7.0 0.7 %copy-done.6 = f32[1,1,2048]{2,1,0:T(1,128)S(1)} copy-done((f32[1,1,2048]{2,1,0:T(1,128)S(1)}, f32[1,1,2048]{2,1,0:T(1,128)}, u32[]{:S(2)}) %copy-start.6) | copy-done | bytes 8216
  7.7 0.0 copy-start.7
  7.7 0.7 %copy-done.7 = f32[1,1,2048]{2,1,0:T(1,128)S(1)} copy-done((f32[1,1,2048]{2,1,0:T(1,128)S(1)}, f32[1,1,2048]{2,1,0:T(1,128)}, u32[]{:S(2)}) %copy-start.7) | copy-done | bytes 8216
  8.4 0.0 copy-start.8
  8.4 0.7 %copy-done.8 = s32[1,1,2048]{2,1,0:T(1,128)S(1)} copy-done((s32[1,1,2048]{2,1,0:T(1,128)S(1)}, s32[1,1,2048]{2,1,0:T(1,128)}, u32[]{:S(2)}) %copy-start.8) | copy-done | bytes 8216
  9.1 37.2 %shard_map.148 = (f32[2,8,64,128]{3,2,1,0:T(8,128)S(1)}, f32[4,2048]{1,0:T(4,128)S(1)}, f32[8,38,128]{2,1,0:T(8,128)S(1)}) custom-call(f32[2,8,64,128]{3,2,1,0:T(8,128)S(1)} %copy-done, f32[2,64,128]{2,1,0:T(8,128)S(1)} %copy-done.2, s32[64,128]{1,0:T(8,128)S(1)} %copy-done.3, f32[2,2048]{1,0:T(2,128)S(1)} %bitcast.18, f32[2,2048]{1,0:T(2,128)S(1)} %bitcast.19, ...), custom_call_target="tpu_custom_call" | custom-call | tf_op jit(solution)/shard_map/pallas_call | solution.py:383
  46.3 0.7 %copy.16 = f32[1,1,8,38,128]{4,2,3,1,0:T(8,128)} copy(f32[1,1,8,38,128]{4,3,2,1,0:T(8,128)S(1)} %bitcast.14) | data formatting | bytes 311296
  47.0 0.8 %copy.23 = f32[2,8,64,128]{3,2,1,0:T(8,128)} copy(f32[2,8,64,128]{3,2,1,0:T(8,128)S(1)} %get-tuple-element.15) | data formatting | bytes 1048576
  47.8 0.6 %copy.24 = f32[1,1,4,2048]{3,2,1,0:T(4,128)} copy(f32[1,1,4,2048]{3,2,1,0:T(4,128)S(1)} %bitcast.15) | data formatting | bytes 65536
Async XLA Ops:
  0.6 1.4 %copy-start.4 = (f32[1,1,2,2048]{3,2,1,0:T(2,128)S(1)}, f32[1,1,2,2048]{3,2,1,0:T(2,128)}, u32[]{:S(2)}) copy-start(f32[1,1,2,2048]{3,2,1,0:T(2,128)} %param.16) | copy-start | bytes 49156
  1.3 0.7 %copy-start.9 = (s32[1,1,8,128]{3,2,1,0:T(8,128)S(1)}, s32[1,1,8,128]{3,2,1,0:T(8,128)}, u32[]{:S(2)}) copy-start(s32[1,1,8,128]{3,2,1,0:T(8,128)} %param.24) | copy-start | bytes 12292
  2.0 0.7 %copy-start.10 = (s32[1,1,8]{2,1,0:T(1,128)S(1)}, s32[1,1,8]{2,1,0:T(1,128)}, u32[]{:S(2)}) copy-start(s32[1,1,8]{2,1,0:T(1,128)} %param.25) | copy-start | bytes 100
  2.7 1.0 %copy-start = (f32[2,8,64,128]{3,2,1,0:T(8,128)S(1)}, f32[2,8,64,128]{3,2,1,0:T(8,128)}, u32[]{:S(2)}) copy-start(f32[2,8,64,128]{3,2,1,0:T(8,128)} %ocean.1) | copy-start | bytes 1572868
  3.7 0.9 %copy-start.1 = (f32[1,1,32,2048]{3,2,1,0:T(8,128)S(1)}, f32[1,1,32,2048]{3,2,1,0:T(8,128)}, u32[]{:S(2)}) copy-start(f32[1,1,32,2048]{3,2,1,0:T(8,128)} %param.20) | copy-start | bytes 786436
  4.6 0.8 %copy-start.2 = (f32[2,64,128]{2,1,0:T(8,128)S(1)}, f32[2,64,128]{2,1,0:T(8,128)}, u32[]{:S(2)}) copy-start(f32[2,64,128]{2,1,0:T(8,128)} %wind.1) | copy-start | bytes 196612
  5.5 0.8 %copy-start.3 = (s32[64,128]{1,0:T(8,128)S(1)}, s32[64,128]{1,0:T(8,128)}, u32[]{:S(2)}) copy-start(s32[64,128]{1,0:T(8,128)} %counts.1) | copy-start | bytes 98308
  6.2 0.7 %copy-start.5 = (f32[1,1,2,2048]{3,2,1,0:T(2,128)S(1)}, f32[1,1,2,2048]{3,2,1,0:T(2,128)}, u32[]{:S(2)}) copy-start(f32[1,1,2,2048]{3,2,1,0:T(2,128)} %param.17) | copy-start | bytes 49156
  7.0 0.7 %copy-start.6 = (f32[1,1,2048]{2,1,0:T(1,128)S(1)}, f32[1,1,2048]{2,1,0:T(1,128)}, u32[]{:S(2)}) copy-start(f32[1,1,2048]{2,1,0:T(1,128)} %param.18) | copy-start | bytes 24580
  7.7 0.7 %copy-start.7 = (f32[1,1,2048]{2,1,0:T(1,128)S(1)}, f32[1,1,2048]{2,1,0:T(1,128)}, u32[]{:S(2)}) copy-start(f32[1,1,2048]{2,1,0:T(1,128)} %param.19) | copy-start | bytes 24580
  8.4 0.7 %copy-start.8 = (s32[1,1,2048]{2,1,0:T(1,128)S(1)}, s32[1,1,2048]{2,1,0:T(1,128)}, u32[]{:S(2)}) copy-start(s32[1,1,2048]{2,1,0:T(1,128)} %param.21) | copy-start | bytes 24580

commit v2 on v1

--- a/solution.py
+++ b/solution.py
@@ -23,7 +23,7 @@
 UP, LEFT, RIGHT, DOWN = 1, 3, 4, 6
 MESH = pl.DeviceIdType.MESH
 f32 = jnp.float32
-UNROLL = 2
+UNROLL = 4
 
 
 def lane_gather(values, lanes):
@@ -35,12 +35,23 @@
 
 
 def kernel(
-    ocean, wind, counts, pos, vel, rad, mass, poly, cells, ccount, clist, clist_v, mindex, mcount,
+    ocean_h, wind_h, counts_h, pos_h, vel_h, rad_h, mass_h, poly_h, cells_h,
+    ccount, clist, clist_v, mindex, mcount,
     ocean_out, floe_out, arrive_out,
     flow, cnt, wnd, halo_o, halo_c, pack, side, corner, edge72, own, gh, cols, forces,
     surf, late_s, early_s, early_r, next_s, next_r,
-    sem_s, sem_r,
+    ocean, wind, counts, pos, vel, rad, mass, poly, cells,
+    sem_s, sem_r, sem_i,
 ):
+    loads = [
+        pltpu.make_async_copy(src, dst, sem_i.at[n])
+        for n, (src, dst) in enumerate((
+            (ocean_h, ocean), (wind_h, wind), (counts_h, counts), (pos_h, pos), (vel_h, vel),
+            (rad_h, rad), (poly_h, poly), (mass_h, mass), (cells_h, cells),
+        ))
+    ]
+    for load in loads:
+        load.start()
     levels, rows, width = ocean.shape[1], ocean.shape[2], ocean.shape[3]
     floes = pos.shape[1]
     blocks = floes // 128
@@ -76,6 +87,8 @@
         def _():
             pl.semaphore_signal(barrier, inc=1, device_id=ids[way], device_id_type=MESH)
 
+    for load in loads[:6]:
+        load.wait()
     for b in range(blocks):
         at = slice(128 * b, 128 * b + 128)
         own[b, 0:2] = pos[:, at]
@@ -134,9 +147,11 @@
         for way, c in copies:
             pl.when(there[way])(c.wait_send)
 
+    start(records)
     start(halo)
-    start(records)
-
+
+    for load in loads[6:]:
+        load.wait()
     lane8 = iota((8, 128), 1)
 
     def gather_early(w, carry):
@@ -162,7 +177,47 @@
         cols[b] = own[b].T
         return carry
 
-    lax.fori_loop(0, blocks, own_cols, 0)
+    lax.fori_loop(0, blocks, own_cols, 0, unroll=8)
+
+    landed(records)
+
+    def ghost_cols(b, carry):
+        cols[blocks + b] = gh[b].T
+        return carry
+
+    lax.fori_loop(0, 8 * GHOST, ghost_cols, 0, unroll=8)
+
+    def contact(t, carry):
+        a, s, c = clist[0, t], clist[1, t], clist[2, t]
+        neighbour = s - (s > 4).astype(jnp.int32)
+        partner = jnp.where(s == 4, c, blocks + neighbour * GHOST + c)
+        partner = jnp.clip(partner, 0, blocks + 8 * GHOST - 1)
+        mine = own[a]
+        other = cols[partner]
+        step = 16
+        xi, yi, ui, vi, ri = [jnp.broadcast_to(mine[f : f + 1], (step, 128)) for f in range(5)]
+        sx = jnp.zeros((step, 128), f32)
+        sy = jnp.zeros((step, 128), f32)
+        for q in range(0, 128, step):
+            xj, yj, uj, vj, rj = [
+                jnp.broadcast_to(other[q : q + step, f : f + 1], (step, 128)) for f in range(5)
+            ]
+            dx, dy = xi - xj, yi - yj
+            square = dx * dx + dy * dy + SOFTEN * SOFTEN
+            inverse = lax.rsqrt(square)
+            reach = ri + rj
+            overlap = jnp.maximum(reach - square * inverse, 0.0)
+            guess = pl.reciprocal(reach, approx=True)
+            reduced = ri * rj * (guess * (2.0 - reach * guess))
+            closing = ((ui - uj) * dx + (vi - vj) * dy) * inverse
+            m = overlap * reduced * (STIFFNESS - DAMPING * closing) * inverse
+            sx = sx + m * dx
+            sy = sy + m * dy
+        forces[0, pl.ds(t, 1)] = jnp.sum(sx, axis=0, keepdims=True)
+        forces[1, pl.ds(t, 1)] = jnp.sum(sy, axis=0, keepdims=True)
+        return carry
+
+    lax.fori_loop(0, slots // 2, contact, 0, unroll=UNROLL)
 
     landed(halo)
     sub8 = iota((8, width), 0)
@@ -263,44 +318,7 @@
 
     lax.fori_loop(0, levels, write, 0)
 
-    landed(records)
-
-    def ghost_cols(b, carry):
-        cols[blocks + b] = gh[b].T
-        return carry
-
-    lax.fori_loop(0, 8 * GHOST, ghost_cols, 0)
-
-    def contact(t, carry):
-        a, s, c = clist[0, t], clist[1, t], clist[2, t]
-        neighbour = s - (s > 4).astype(jnp.int32)
-        partner = jnp.where(s == 4, c, blocks + neighbour * GHOST + c)
-        partner = jnp.clip(partner, 0, blocks + 8 * GHOST - 1)
-        mine = own[a]
-        other = cols[partner]
-        step = 16
-        xi, yi, ui, vi, ri = [jnp.broadcast_to(mine[f : f + 1], (step, 128)) for f in range(5)]
-        sx = jnp.zeros((step, 128), f32)
-        sy = jnp.zeros((step, 128), f32)
-        for q in range(0, 128, step):
-            xj, yj, uj, vj, rj = [
-                jnp.broadcast_to(other[q : q + step, f : f + 1], (step, 128)) for f in range(5)
-            ]
-            dx, dy = xi - xj, yi - yj
-            square = dx * dx + dy * dy + SOFTEN * SOFTEN
-            inverse = lax.rsqrt(square)
-            reach = ri + rj
-            overlap = jnp.maximum(reach - square * inverse, 0.0)
-            reduced = ri * rj / reach
-            closing = ((ui - uj) * dx + (vi - vj) * dy) * inverse
-            m = overlap * reduced * (STIFFNESS - DAMPING * closing) * inverse
-            sx = sx + m * dx
-            sy = sy + m * dy
-        forces[0, pl.ds(t, 1)] = jnp.sum(sx, axis=0, keepdims=True)
-        forces[1, pl.ds(t, 1)] = jnp.sum(sy, axis=0, keepdims=True)
-        return carry
-
-    lax.fori_loop(0, slots, contact, 0, unroll=UNROLL)
+    lax.fori_loop(slots // 2, slots, contact, 0, unroll=UNROLL)
     takes = (iota((blocks, slots), 0) == clist_v[0:1]) & (iota((blocks, slots), 1) < ccount[0, 0])
     takes = takes.astype(f32)
     push = [
@@ -387,7 +405,7 @@
             jax.ShapeDtypeStruct((4, floes), f32),
             jax.ShapeDtypeStruct((8, fields, 128), f32),
         ),
-        in_specs=[vmem] * 9 + [smem, smem, vmem, vmem, smem],
+        in_specs=[pl.BlockSpec(memory_space=pltpu.HBM)] * 9 + [smem, smem, vmem, vmem, smem],
         out_specs=(vmem, vmem, vmem),
         scratch_shapes=[
             pltpu.VMEM((2, levels, ext, width), f32),
@@ -409,11 +427,21 @@
             pltpu.VMEM((8, 40, 128), f32),
             pltpu.VMEM((8, 8, 128), f32),
             pltpu.VMEM((8, 8, 128), f32),
+            pltpu.VMEM(ocean_velocity.shape, f32),
+            pltpu.VMEM(wind_stress.shape, f32),
+            pltpu.VMEM(level_counts.shape, jnp.int32),
+            pltpu.VMEM((2, floes), f32),
+            pltpu.VMEM((2, floes), f32),
+            pltpu.VMEM((1, floes), f32),
+            pltpu.VMEM((1, floes), f32),
+            pltpu.VMEM(floe_polygon.shape[2:], f32),
+            pltpu.VMEM((1, floes), jnp.int32),
             pltpu.SemaphoreType.DMA((40,)),
             pltpu.SemaphoreType.DMA((40,)),
+            pltpu.SemaphoreType.DMA((9,)),
         ],
         compiler_params=pltpu.CompilerParams(
-            collective_id=0, has_side_effects=True, vmem_limit_bytes=40 * 1024 * 1024
+            collective_id=0, has_side_effects=True, vmem_limit_bytes=60 * 1024 * 1024
         ),
     )(
         ocean_velocity, wind_stress, level_counts, floe_position[0, 0], floe_velocity[0, 0],

time: 49 us -> 40.1 us (0.82)
  local copies, waits for them, and re-layouts: 9.84 us -> 5.37 us
  Pallas kernels: 37.2 us -> 33.1 us
    unnamed x26 -> x8, local copies, waits for them, and re-layouts: 9.84 us -> 5.37 us
    pallas_call x1, Pallas kernels: 37.2 us -> 33.1 us  [shards(): pl.pallas_call(kernel, out_shape=(jax.ShapeDtypeStruct(ocean_velocity.sha...]
where the time goes in v2:
time: 40.1 us; the launch traced here: 39.7 us
  Pallas kernels  33.1 us (83%)
  local copies, waits for them, and re-layouts  5.37 us (13%)
  between operations  1.3 us (3%)
    pallas_call x1, Pallas kernels, shards(): pl.pallas_call(kernel, out_shape=(jax.ShapeDtypeStruct(ocean_velocity.sha...  33.1 us
    unnamed x8, local copies, waits for them, and re-layouts  5.37 us

profile of v2, /device:TPU:1, one launch (start us, length us, event | category | flops | bytes accessed | tf_op | source)
XLA Modules:
  0.0 39.7 jit_solution(10756981691386414408)
XLA Ops:
  1.3 0.0 copy-start.1
  1.3 0.7 %copy-done.1 = s32[1,1,3,64]{3,1,2,0:T(1,128)S(1)} copy-done((s32[1,1,3,64]{3,1,2,0:T(1,128)S(1)}, s32[1,1,3,64]{3,1,2,0:T(1,128)}, u32[]{:S(2)}) %copy-start.1) | copy-done | bytes 792
  2.0 0.6 %copy.19 = s32[1,1,3,64]{3,2,1,0:T(4,128)} copy(s32[1,1,3,64]{3,1,2,0:T(1,128)S(1)} %copy-done.1) | data formatting | bytes 1536
  2.5 33.1 %shard_map.148 = (f32[2,8,64,128]{3,2,1,0:T(8,128)}, f32[4,2048]{1,0:T(4,128)}, f32[8,38,128]{2,1,0:T(8,128)}) custom-call(f32[2,8,64,128]{3,2,1,0:T(8,128)} %ocean_h.1, f32[2,64,128]{2,1,0:T(8,128)} %wind_h.1, s32[64,128]{1,0:T(8,128)} %counts_h.1, f32[2,2048]{1,0:T(2,128)} %bitcast.18, f32[2,2048]{1,0:T(2,128)} %bitcast.19, f32[1,2048]{1,0:T(1,128)} %bitcast.20, ...), custom_call_target="tpu_custom_call" | custom-call | tf_op jit(solution)/shard_map/pallas_call | solution.py:401
  35.6 1.6 %copy.16 = f32[1,1,8,38,128]{4,2,3,1,0:T(8,128)} copy(f32[1,1,8,38,128]{4,3,2,1,0:T(8,128)} %bitcast.14) | data formatting | bytes 311296
  37.2 0.0 copy-start
  37.2 1.9 %copy.23 = f32[2,8,64,128]{3,2,1,0:T(8,128)} copy(f32[2,8,64,128]{3,2,1,0:T(8,128)} %get-tuple-element.15) | data formatting | bytes 1048576
  39.1 0.0 copy-done
  39.1 0.6 %copy.24 = f32[1,1,4,2048]{3,2,1,0:T(4,128)} copy(f32[1,1,4,2048]{3,2,1,0:T(4,128)S(1)} %bitcast.15) | data formatting | bytes 65536
Async XLA Ops:
  1.3 0.7 %copy-start.1 = (s32[1,1,3,64]{3,1,2,0:T(1,128)S(1)}, s32[1,1,3,64]{3,1,2,0:T(1,128)}, u32[]{:S(2)}) copy-start(s32[1,1,3,64]{3,1,2,0:T(1,128)} %param.23) | copy-start | bytes 2308
  37.2 1.9 %copy-start = (f32[4,2048]{1,0:T(4,128)S(1)}, f32[4,2048]{1,0:T(4,128)}, u32[]{:S(2)}) copy-start(f32[4,2048]{1,0:T(4,128)} %get-tuple-element.7) | copy-start | bytes 98308

commit v3 on v2

--- a/solution.py
+++ b/solution.py
@@ -194,7 +194,7 @@
         partner = jnp.clip(partner, 0, blocks + 8 * GHOST - 1)
         mine = own[a]
         other = cols[partner]
-        step = 16
+        step = 64
         xi, yi, ui, vi, ri = [jnp.broadcast_to(mine[f : f + 1], (step, 128)) for f in range(5)]
         sx = jnp.zeros((step, 128), f32)
         sy = jnp.zeros((step, 128), f32)
@@ -287,7 +287,7 @@
             return tuple(new_fluxes)
 
         nothing = jnp.zeros((ext, width), f32)
-        lax.fori_loop(0, levels, level, (nothing, nothing))
+        lax.fori_loop(0, levels, level, (nothing, nothing), unroll=2)
         hp = 0.15 - 0.05 * level_f / levels
         turn_by = jnp.where(lane72 < 64, CORIOLIS, -CORIOLIS)
         for which in range(2):
@@ -311,12 +311,8 @@
     for c in range(2):
         surf[c, margin : margin + rows] = late_s[c]
 
-    def write(k, carry):
-        for c in range(2):
-            ocean_out[c, k] = flow[c, k, 0:rows]
-        return carry
-
-    lax.fori_loop(0, levels, write, 0)
+    store = pltpu.make_async_copy(flow.at[:, :, pl.ds(0, rows)], ocean_out, sem_i.at[9])
+    store.start()
 
     lax.fori_loop(slots // 2, slots, contact, 0, unroll=UNROLL)
     takes = (iota((blocks, slots), 0) == clist_v[0:1]) & (iota((blocks, slots), 1) < ccount[0, 0])
@@ -383,6 +379,7 @@
         arrive_out[w, 0:4] = next_r[w, 0:4]
     for copies in (halo, records, early, strips, late):
         sent(copies)
+    store.wait()
 
 
 def shards(
@@ -406,7 +403,7 @@
             jax.ShapeDtypeStruct((8, fields, 128), f32),
         ),
         in_specs=[pl.BlockSpec(memory_space=pltpu.HBM)] * 9 + [smem, smem, vmem, vmem, smem],
-        out_specs=(vmem, vmem, vmem),
+        out_specs=(pl.BlockSpec(memory_space=pltpu.HBM), vmem, vmem),
         scratch_shapes=[
             pltpu.VMEM((2, levels, ext, width), f32),
             pltpu.VMEM((ext, width), f32),
@@ -438,7 +435,7 @@
             pltpu.VMEM((1, floes), jnp.int32),
             pltpu.SemaphoreType.DMA((40,)),
             pltpu.SemaphoreType.DMA((40,)),
-            pltpu.SemaphoreType.DMA((9,)),
+            pltpu.SemaphoreType.DMA((10,)),
         ],
         compiler_params=pltpu.CompilerParams(
             collective_id=0, has_side_effects=True, vmem_limit_bytes=60 * 1024 * 1024

time: 40.1 us -> 37 us (0.923)
  Pallas kernels: 33.1 us -> 29.9 us
    pallas_call x1, Pallas kernels: 33.1 us -> 29.9 us  [shards(): pl.pallas_call(kernel, out_shape=(jax.ShapeDtypeStruct(ocean_velocity.sha...]
where the time goes in v3:
time: 37 us; the launch traced here: 36.6 us
  Pallas kernels  29.9 us (81%)
  local copies, waits for them, and re-layouts  5.37 us (15%)
  between operations  1.3 us (4%)
    pallas_call x1, Pallas kernels, shards(): pl.pallas_call(kernel, out_shape=(jax.ShapeDtypeStruct(ocean_velocity.sha...  29.9 us
    unnamed x8, local copies, waits for them, and re-layouts  5.37 us

profile of v3, /device:TPU:1, one launch (start us, length us, event | category | flops | bytes accessed | tf_op | source)
XLA Modules:
  0.0 36.6 jit_solution(15815273172066448653)
XLA Ops:
  1.3 0.0 copy-start.1
  1.3 0.7 %copy-done.1 = s32[1,1,3,64]{3,1,2,0:T(1,128)S(1)} copy-done((s32[1,1,3,64]{3,1,2,0:T(1,128)S(1)}, s32[1,1,3,64]{3,1,2,0:T(1,128)}, u32[]{:S(2)}) %copy-start.1) | copy-done | bytes 792
  2.0 0.6 %copy.19 = s32[1,1,3,64]{3,2,1,0:T(4,128)} copy(s32[1,1,3,64]{3,1,2,0:T(1,128)S(1)} %copy-done.1) | data formatting | bytes 1536
  2.5 29.9 %shard_map.148 = (f32[2,8,64,128]{3,2,1,0:T(8,128)}, f32[4,2048]{1,0:T(4,128)}, f32[8,38,128]{2,1,0:T(8,128)}) custom-call(f32[2,8,64,128]{3,2,1,0:T(8,128)} %ocean_h.1, f32[2,64,128]{2,1,0:T(8,128)} %wind_h.1, s32[64,128]{1,0:T(8,128)} %counts_h.1, f32[2,2048]{1,0:T(2,128)} %bitcast.18, f32[2,2048]{1,0:T(2,128)} %bitcast.19, f32[1,2048]{1,0:T(1,128)} %bitcast.20, ...), custom_call_target="tpu_custom_call" | custom-call | tf_op jit(solution)/shard_map/pallas_call | solution.py:398
  32.5 1.6 %copy.16 = f32[1,1,8,38,128]{4,2,3,1,0:T(8,128)} copy(f32[1,1,8,38,128]{4,3,2,1,0:T(8,128)} %bitcast.14) | data formatting | bytes 311296
  34.1 0.0 copy-start
  34.1 1.9 %copy.23 = f32[2,8,64,128]{3,2,1,0:T(8,128)} copy(f32[2,8,64,128]{3,2,1,0:T(8,128)} %get-tuple-element.15) | data formatting | bytes 1048576
  36.0 0.0 copy-done
  36.0 0.6 %copy.24 = f32[1,1,4,2048]{3,2,1,0:T(4,128)} copy(f32[1,1,4,2048]{3,2,1,0:T(4,128)S(1)} %bitcast.15) | data formatting | bytes 65536
Async XLA Ops:
  1.3 0.7 %copy-start.1 = (s32[1,1,3,64]{3,1,2,0:T(1,128)S(1)}, s32[1,1,3,64]{3,1,2,0:T(1,128)}, u32[]{:S(2)}) copy-start(s32[1,1,3,64]{3,1,2,0:T(1,128)} %param.23) | copy-start | bytes 2308
  34.1 1.9 %copy-start = (f32[4,2048]{1,0:T(4,128)S(1)}, f32[4,2048]{1,0:T(4,128)}, u32[]{:S(2)}) copy-start(f32[4,2048]{1,0:T(4,128)} %get-tuple-element.7) | copy-start | bytes 98308
